TPU v7x, 256 devices: a whole 4x4x8 slice. The times are simulated.
256 devices in a mesh: gx: 32 (over y, z), gy: 8 (over x, core).
Axes of the slice: x: 4, y: 4, z: 8, core: 2. Of those that a mesh axis runs over, the one named last changes fastest.
Arguments:
- right_side: float32 [512, 256, 256], P('gx', 'gy'), may hold values from -8 to 8
- coefficient: float32 [64, 32, 32], P('gx', 'gy'), may hold values from 0.2 to 5
Outputs:
- solution_field: float32 [512, 256, 256], P('gx', 'gy')
- residual: float32 [512, 256, 256], P('gx', 'gy')
All inputs are finite; a program needn't handle non-finite values.
Results may differ from a plain program's by a relative error of at most 0.0003.
Values sent between devices are 32-bit elements; how exact they have to be, the bound alone decides.
A program may use at most 128 MiB of HBM per device.

v0:
```python
import math

import jax
import jax.numpy as jnp
import numpy as np
from jax import lax
from jax.sharding import PartitionSpec as P

ORDER = 7
COARSE_ORDER = 3
ITERS = 2


def with_halo(array, sides, width):
    for axis, dim in sides:
        peers, length = (lax.axis_size(axis), array.shape[dim])
        up = [(i, (i + 1) % peers) for i in range(peers - 1)]
        down = [(j, i) for i, j in up]
        last = lax.slice_in_dim(array, length - width, length, axis=dim)
        first = lax.slice_in_dim(array, 0, width, axis=dim)
        before = lax.ppermute(last, axis, up)
        after = lax.ppermute(first, axis, down)
        array = jnp.concatenate([before, array, after], axis=dim)
    return array


def legendre_pair(degree, points):
    before = points * 0.0 + 1.0
    now = points.copy()
    for power in range(2, degree + 1):
        after = ((2 * power - 1) * points * now - (power - 1) * before) / power
        before = now
        now = after
    return (now, before)


def gll_tables(degree):
    number = degree + 1
    points = np.cos(math.pi * np.arange(number) / degree)
    for newton in range(60):
        top, below = legendre_pair(degree, points)
        points = points - (points * top - below) / (number * top)
    points = points[::-1].copy()
    points[0] = -1.0
    points[degree] = 1.0
    values = legendre_pair(degree, points)[0]
    weights = 2.0 / (degree * (degree + 1) * values**2)
    derivative = np.zeros((number, number))
    for row_index in range(number):
        for column_index in range(number):
            if row_index != column_index:
                derivative[row_index, column_index] = values[row_index] / (
                    values[column_index] * (points[row_index] - points[column_index])
                )
    derivative[0, 0] = -degree * (degree + 1) / 4.0
    derivative[degree, degree] = degree * (degree + 1) / 4.0
    stiffness = derivative.T @ (weights[:, None] * derivative)
    return (points, weights, stiffness)


def main_diagonal(matrix):
    return np.array([matrix[index, index] for index in range(matrix.shape[0])])


def upper_bound(degree):
    points, weights, stiffness = gll_tables(degree)
    rowsum = np.abs(stiffness).sum(1)
    diagonal = main_diagonal(stiffness)
    top = rowsum[:, None, None] * weights[None, :, None] * weights[None, None, :]
    top = top + weights[:, None, None] * rowsum[None, :, None] * weights[None, None, :]
    top = top + weights[:, None, None] * weights[None, :, None] * rowsum[None, None, :]
    bottom = diagonal[:, None, None] * weights[None, :, None] * weights[None, None, :]
    bottom = bottom + weights[:, None, None] * diagonal[None, :, None] * weights[None, None, :]
    bottom = bottom + weights[:, None, None] * weights[None, :, None] * diagonal[None, None, :]
    return float((top / bottom).max())


def interpolation_matrix(fine_degree, coarse_degree):
    fine_points = gll_tables(fine_degree)[0]
    coarse_points = gll_tables(coarse_degree)[0]
    matrix = np.ones((fine_degree + 1, coarse_degree + 1))
    for column_index in range(coarse_degree + 1):
        for other_index in range(coarse_degree + 1):
            if other_index != column_index:
                matrix[:, column_index] *= (fine_points - coarse_points[other_index]) / (
                    coarse_points[column_index] - coarse_points[other_index]
                )
    return matrix


def along_first(field, matrix):
    rows_out, rows_in = matrix.shape
    elements = field.shape[0] // rows_in
    shaped = field.reshape(elements, rows_in, field.shape[1], field.shape[2])
    result = jnp.einsum("ai,xiyz->xayz", matrix, shaped, precision=lax.Precision.HIGHEST)
    return result.reshape(elements * rows_out, field.shape[1], field.shape[2])


def along_second(field, matrix):
    rows_out, rows_in = matrix.shape
    elements = field.shape[1] // rows_in
    shaped = field.reshape(field.shape[0], elements, rows_in, field.shape[2])
    result = jnp.einsum("ai,xeiz->xeaz", matrix, shaped, precision=lax.Precision.HIGHEST)
    return result.reshape(field.shape[0], elements * rows_out, field.shape[2])


def along_third(field, matrix):
    rows_out, rows_in = matrix.shape
    elements = field.shape[2] // rows_in
    group = math.gcd(elements, max(1, 128 // rows_out))
    block = jnp.kron(jnp.eye(group, dtype=jnp.float32), matrix)
    shaped = field.reshape(field.shape[0], field.shape[1], elements // group, group * rows_in)
    result = jnp.einsum("xyqi,ai->xyqa", shaped, block, precision=lax.Precision.HIGHEST)
    return result.reshape(field.shape[0], field.shape[1], elements * rows_out)


def apply_dims(field, matrix):
    return along_third(along_second(along_first(field, matrix), matrix), matrix)


def sum_first(padded, number):
    rows = padded.shape[0] - 2
    position = jnp.arange(rows) % number
    upper = (position == number - 1).astype(jnp.float32)[:, None, None]
    lower = (position == 0).astype(jnp.float32)[:, None, None]
    return padded[1:-1] + upper * padded[2:] + lower * padded[:-2]


def sum_second(padded, number):
    columns = padded.shape[1] - 2
    position = jnp.arange(columns) % number
    upper = (position == number - 1).astype(jnp.float32)[None, :, None]
    lower = (position == 0).astype(jnp.float32)[None, :, None]
    return padded[:, 1:-1] + upper * padded[:, 2:] + lower * padded[:, :-2]


def sum_third(field, number):
    padded = jnp.pad(field, ((0, 0), (0, 0), (1, 1)))
    depth = field.shape[2]
    position = jnp.arange(depth) % number
    upper = (position == number - 1).astype(jnp.float32)[None, None, :]
    lower = (position == 0).astype(jnp.float32)[None, None, :]
    return padded[:, :, 1:-1] + upper * padded[:, :, 2:] + lower * padded[:, :, :-2]


def node_masks(count, offset, total, number):
    index = offset + jnp.arange(count, dtype=jnp.int32)
    inside = ((index != 0) & (index != total - 1)).astype(jnp.float32)
    upper = ((index % number == number - 1) & (index != total - 1)).astype(jnp.float32)
    lower = ((index % number == 0) & (index != 0)).astype(jnp.float32)
    return (inside, 1.0 + upper + lower)


def build_level(degree, coefficient, offsets, totals, summation):
    points, weights_np, stiffness_np = gll_tables(degree)
    number = degree + 1
    weights = jnp.asarray(weights_np, dtype=jnp.float32)
    stiffness = jnp.asarray(stiffness_np, dtype=jnp.float32)
    diagonal = jnp.asarray(main_diagonal(stiffness_np), dtype=jnp.float32)
    counts = [
        coefficient.shape[0] * number,
        coefficient.shape[1] * number,
        coefficient.shape[2] * number,
    ]
    tiled = [jnp.tile(weights, coefficient.shape[dim_index]) for dim_index in range(3)]
    tiled_diag = [jnp.tile(diagonal, coefficient.shape[dim_index]) for dim_index in range(3)]
    coeff_nodes = jnp.repeat(jnp.repeat(jnp.repeat(coefficient, number, 0), number, 1), number, 2)
    first = node_masks(counts[0], offsets[0], totals[0], number)
    second = node_masks(counts[1], offsets[1], totals[1], number)
    third = node_masks(counts[2], offsets[2], totals[2], number)
    mask = first[0][:, None, None] * second[0][None, :, None] * third[0][None, None, :]
    weight_inv = 1.0 / (
        first[1][:, None, None] * second[1][None, :, None] * third[1][None, None, :]
    )
    wx = tiled[0][:, None, None]
    wy = tiled[1][None, :, None]
    wz = tiled[2][None, None, :]
    local_diag = coeff_nodes * (
        tiled_diag[0][:, None, None] * wy * wz
        + wx * tiled_diag[1][None, :, None] * wz
        + wx * wy * tiled_diag[2][None, None, :]
    )
    dinv = mask / summation(local_diag)
    return {
        "stiffness": stiffness,
        "wx": wx,
        "wy": wy,
        "wz": wz,
        "coeff_nodes": coeff_nodes,
        "mask": mask,
        "weight_inv": weight_inv,
        "dinv": dinv,
        "upper": upper_bound(degree),
        "summation": summation,
    }


def local_stiffness(level, field):
    stiffness = level["stiffness"]
    first = along_first(field, stiffness) * (level["wy"] * level["wz"])
    second = along_second(field, stiffness) * (level["wx"] * level["wz"])
    third = along_third(field, stiffness) * (level["wx"] * level["wy"])
    return level["coeff_nodes"] * (first + second + third)


def apply_operator(level, field):
    return level["mask"] * level["summation"](local_stiffness(level, field))


def chebyshev(level, rhs_field, start):
    upper = level["upper"]
    lower = 0.1 * upper
    center = 0.5 * (upper + lower)
    halfwidth = 0.5 * (upper - lower)
    if start is None:
        remain = rhs_field
        change = level["dinv"] * remain / center
        result = change
    else:
        remain = rhs_field - apply_operator(level, start)
        change = level["dinv"] * remain / center
        result = start + change
    previous = halfwidth / center
    remain = remain - apply_operator(level, change)
    current = 1.0 / (2.0 * center / halfwidth - previous)
    change = current * previous * change + 2.0 * current / halfwidth * level["dinv"] * remain
    result = result + change
    return result


def vcycle(fine, coarse, prolong, restrict, rhs_field):
    smoothed = chebyshev(fine, rhs_field, None)
    defect = rhs_field - apply_operator(fine, smoothed)
    coarse_rhs = coarse["mask"] * coarse["summation"](
        apply_dims(fine["weight_inv"] * defect, restrict)
    )
    coarse_fix = chebyshev(coarse, coarse_rhs, None)
    smoothed = smoothed + apply_dims(coarse_fix, prolong)
    return chebyshev(fine, rhs_field, smoothed)


def fine_summation(field):
    number = ORDER + 1
    padded = with_halo(field, (("gx", 0), ("gy", 1)), 1)
    summed = sum_second(sum_first(padded, number), number)
    return sum_third(summed, number)


def coarse_summation(field):
    number = COARSE_ORDER + 1
    padded = with_halo(field, (("gx", 0), ("gy", 1)), 1)
    summed = sum_second(sum_first(padded, number), number)
    return sum_third(summed, number)


def level_frame(coefficient, number):
    counts = (
        coefficient.shape[0] * number,
        coefficient.shape[1] * number,
        coefficient.shape[2] * number,
    )
    offsets = (lax.axis_index("gx") * counts[0], lax.axis_index("gy") * counts[1], 0)
    totals = (counts[0] * lax.axis_size("gx"), counts[1] * lax.axis_size("gy"), counts[2])
    return (offsets, totals)


def per_device(right_side, coefficient):
    fine_offsets, fine_totals = level_frame(coefficient, ORDER + 1)
    coarse_offsets, coarse_totals = level_frame(coefficient, COARSE_ORDER + 1)
    fine = build_level(ORDER, coefficient, fine_offsets, fine_totals, fine_summation)
    coarse = build_level(COARSE_ORDER, coefficient, coarse_offsets, coarse_totals, coarse_summation)
    prolong_np = interpolation_matrix(ORDER, COARSE_ORDER)
    prolong = jnp.asarray(prolong_np, dtype=jnp.float32)
    restrict = jnp.asarray(prolong_np.T, dtype=jnp.float32)
    weight_inv = fine["weight_inv"]
    solution_field = jnp.zeros_like(right_side)
    residual = fine["mask"] * fine["summation"](right_side)
    direction = residual
    rz_old = jnp.float32(1.0)
    for step_index in range(ITERS):
        precond = vcycle(fine, coarse, prolong, restrict, residual)
        rz_now = lax.psum(jnp.sum(residual * precond * weight_inv), ("gx", "gy"))
        if step_index == 0:
            direction = precond
        else:
            direction = precond + rz_now / rz_old * direction
        image = apply_operator(fine, direction)
        curvature = lax.psum(jnp.sum(direction * image * weight_inv), ("gx", "gy"))
        step_size = rz_now / curvature
        solution_field = solution_field + step_size * direction
        residual = residual - step_size * image
        rz_old = rz_now
    return (solution_field, residual)


def solution(mesh):
    in_specs = (P("gx", "gy", None), P("gx", "gy", None))
    out_specs = (P("gx", "gy", None), P("gx", "gy", None))
    return jax.shard_map(
        per_device, mesh=mesh, in_specs=in_specs, out_specs=out_specs, check_vma=False
    )
```

profile of v0, /device:TPU:1, one launch (start us, length us, event | category | flops | bytes accessed | tf_op | source)
XLA Modules:
  0.0 595.6 jit_solution(9208043993074691256)
XLA Ops:
  2.7 5.0 collective-permute-start
  14.1 4.1 collective-permute-start.12
  25.9 4.0 collective-permute-start.4
  39.4 4.9 collective-permute-start.2
  46.3 3.6 collective-permute-start.6
  59.3 4.7 collective-permute-start.8
  65.4 3.6 collective-permute-done.9
  74.1 3.1 collective-permute-done.11
  80.7 4.8 collective-permute-start.16
  86.8 4.8 collective-permute-done.17
  96.8 3.2 reshape.1138
  105.9 4.9 collective-permute-start.20
  112.8 3.9 collective-permute-start.14
  118.7 3.6 collective-permute-start.22
  128.7 4.3 collective-permute-start.24
  134.3 3.4 collective-permute-done.25
  137.7 3.1 collective-permute-start.26
  150.2 3.6 collective-permute-start.28
  155.2 3.4 collective-permute-done.29
  158.7 3.3 collective-permute-start.30
  170.4 4.7 collective-permute-start.32
  176.3 3.6 collective-permute-done.33
  185.0 3.1 collective-permute-done.35
  191.6 3.7 collective-permute-start.36
  196.7 3.6 collective-permute-done.37
  205.3 3.1 collective-permute-done.39
  210.5 82.3 %all-reduce.17 = (f32[]{:T(128)}, f32[]{:T(128)}) all-reduce(f32[]{:T(128)} %get-tuple-element.7, f32[]{:T(128)} %get-tuple-element.6), channel_id=1, replica_groups=mesh['gx'=32,'gy'=8] {'gx','gy'}, use_global_device_ids=true, to_apply=%region_1.2 | all-reduce | flops 2 | bytes 16 | tf_op jit(solution)/shard_map/psum | solution.py:282
  299.9 3.3 collective-permute-done.41
  303.3 4.2 collective-permute-start.42
  320.0 3.3 collective-permute-done.45
  323.4 3.4 collective-permute-start.46
  328.7 3.1 collective-permute-done.47
  334.9 4.2 collective-permute-start.48
  340.4 3.2 collective-permute-done.49
  343.6 3.3 collective-permute-start.50
  353.1 3.5 collective-permute-start.52
  357.9 3.1 collective-permute-done.53
  361.0 3.4 collective-permute-start.54
  380.6 3.3 collective-permute-done.57
  384.0 3.4 collective-permute-start.58
  400.3 3.3 collective-permute-done.61
  403.7 3.4 collective-permute-start.62
  409.0 3.1 collective-permute-done.63
  414.2 80.0 %psum.30 = f32[]{:T(128)} all-reduce(f32[]{:T(128)} %get-tuple-element.12), channel_id=1, replica_groups=mesh['gx'=32,'gy'=8] {'gx','gy'}, use_global_device_ids=true, to_apply=%region_5.6 | all-reduce | flops 1 | bytes 8 | tf_op jit(solution)/shard_map/psum | solution.py:282
  501.0 3.3 collective-permute-done.65
  504.3 3.9 collective-permute-start.66
  510.2 3.1 collective-permute-done.67
  514.9 77.4 %psum.31 = f32[]{:T(128)} all-reduce(f32[]{:T(128)} %get-tuple-element.10), channel_id=1, replica_groups=mesh['gx'=32,'gy'=8] {'gx','gy'}, use_global_device_ids=true, to_apply=%region_7.8 | all-reduce | flops 1 | bytes 8 | tf_op jit(solution)/shard_map/psum | solution.py:288
  (495 shorter events, 181.4 us)
Async XLA Ops:
  1.4 38.0 %collective-permute-start.1 = (f32[1,32,256]{2,1,0:T(8,128)S(1)}, f32[1,32,256]{2,1,0:T(8,128)S(1)}, u32[]{:S(2)}, u32[]{:S(2)}) collective-permute-start(f32[1,32,256]{2,1,0:T(8,128)S(1)} %get-tuple-element.73), channel_id=1, source_target_pairs={{8,0},{16,8},{24,16},{32,24},{40,32},{48,40},{56,48},{64,56},{72,6... | collective-permute-start | bytes 98312 | tf_op jit(solution)/shard_map/ppermute | solution.py:22
  2.7 35.3 %collective-permute-start = (f32[1,32,256]{2,1,0:T(8,128)S(1)}, f32[1,32,256]{2,1,0:T(8,128)S(1)}, u32[]{:S(2)}, u32[]{:S(2)}) collective-permute-start(f32[1,32,256]{2,1,0:T(8,128)S(1)} %get-tuple-element.74), channel_id=1, source_target_pairs={{0,8},{8,16},{16,24},{24,32},{32,40},{40,48},{48,56},{56,64},{64,7... | collective-permute-start | bytes 98312 | tf_op jit(solution)/shard_map/ppermute | solution.py:21
  14.1 98.0 %collective-permute-start.12 = (f32[1,16,128]{2,1,0:T(8,128)}, f32[1,16,128]{2,1,0:T(8,128)}, u32[]{:S(2)}, u32[]{:S(2)}) collective-permute-start(f32[1,16,128]{2,1,0:T(8,128)} %get-tuple-element.95), channel_id=1, source_target_pairs={{0,8},{8,16},{16,24},{24,32},{32,40},{40,48},{48,56},{56,64},{64,7... | collective-permute-start | bytes 24584 | tf_op jit(solution)/shard_map/ppermute | solution.py:21
  18.2 93.9 %collective-permute-start.13 = (f32[1,16,128]{2,1,0:T(8,128)}, f32[1,16,128]{2,1,0:T(8,128)}, u32[]{:S(2)}, u32[]{:S(2)}) collective-permute-start(f32[1,16,128]{2,1,0:T(8,128)} %get-tuple-element.96), channel_id=1, source_target_pairs={{8,0},{16,8},{24,16},{32,24},{40,32},{48,40},{56,48},{64,56},{72,6... | collective-permute-start | bytes 24584 | tf_op jit(solution)/shard_map/ppermute | solution.py:22
  25.9 18.5 %collective-permute-start.4 = (f32[1,32,256]{2,1,0:T(8,128)S(1)}, f32[1,32,256]{2,1,0:T(8,128)S(1)}, u32[]{:S(2)}, u32[]{:S(2)}) collective-permute-start(f32[1,32,256]{2,1,0:T(8,128)S(1)} %get-tuple-element.75), channel_id=1, source_target_pairs={{0,8},{8,16},{16,24},{24,32},{32,40},{40,48},{48,56},{56,64},{64,7... | collective-permute-start | bytes 98312 | tf_op jit(solution)/shard_map/ppermute | solution.py:21
  38.0 8.3 %collective-permute-start.5 = (f32[1,32,256]{2,1,0:T(8,128)S(1)}, f32[1,32,256]{2,1,0:T(8,128)S(1)}, u32[]{:S(2)}, u32[]{:S(2)}) collective-permute-start(f32[1,32,256]{2,1,0:T(8,128)S(1)} %get-tuple-element.76), channel_id=1, source_target_pairs={{8,0},{16,8},{24,16},{32,24},{40,32},{48,40},{56,48},{64,56},{72,6... | collective-permute-start | bytes 98312 | tf_op jit(solution)/shard_map/ppermute | solution.py:22
  39.4 10.5 %collective-permute-start.2 = (f32[18,1,256]{2,1,0:T(1,128)S(1)}, f32[18,1,256]{2,1,0:T(1,128)S(1)}, u32[]{:S(2)}, u32[]{:S(2)}) collective-permute-start(f32[18,1,256]{2,1,0:T(1,128)S(1)} %get-tuple-element.49), channel_id=1, source_target_pairs={{0,1},{1,2},{2,3},{3,4},{4,5},{5,6},{6,7},{8,9},{9,10},{10,11},{11... | collective-permute-start | bytes 55304 | tf_op jit(solution)/shard_map/ppermute | solution.py:21
  44.4 7.6 %collective-permute-start.3 = (f32[18,1,256]{2,1,0:T(1,128)S(1)}, f32[18,1,256]{2,1,0:T(1,128)S(1)}, u32[]{:S(2)}, u32[]{:S(2)}) collective-permute-start(f32[18,1,256]{2,1,0:T(1,128)S(1)} %get-tuple-element.50), channel_id=1, source_target_pairs={{1,0},{2,1},{3,2},{4,3},{5,4},{6,5},{7,6},{9,8},{10,9},{11,10},{12... | collective-permute-start | bytes 55304 | tf_op jit(solution)/shard_map/ppermute | solution.py:22
  46.3 5.7 collective-permute-start.6
  50.0 5.1 collective-permute-start.7
  59.3 6.1 %collective-permute-start.8 = (f32[1,32,256]{2,1,0:T(8,128)S(1)}, f32[1,32,256]{2,1,0:T(8,128)S(1)}, u32[]{:S(2)}, u32[]{:S(2)}) collective-permute-start(f32[1,32,256]{2,1,0:T(8,128)S(1)} %get-tuple-element.71), channel_id=1, source_target_pairs={{0,8},{8,16},{16,24},{24,32},{32,40},{40,48},{48,56},{56,64},{64,7... | collective-permute-start | bytes 98312 | tf_op jit(solution)/shard_map/ppermute | solution.py:21
  69.1 5.1 collective-permute-start.10
  72.2 5.1 collective-permute-start.11
  80.7 6.1 %collective-permute-start.16 = (f32[1,32,256]{2,1,0:T(8,128)S(1)}, f32[1,32,256]{2,1,0:T(8,128)S(1)}, u32[]{:S(2)}, u32[]{:S(2)}) collective-permute-start(f32[1,32,256]{2,1,0:T(8,128)S(1)} %get-tuple-element.69), channel_id=1, source_target_pairs={{0,8},{8,16},{16,24},{24,32},{32,40},{40,48},{48,56},{56,64},{64,7... | collective-permute-start | bytes 98312 | tf_op jit(solution)/shard_map/ppermute | solution.py:21
  85.4 6.2 %collective-permute-start.17 = (f32[1,32,256]{2,1,0:T(8,128)S(1)}, f32[1,32,256]{2,1,0:T(8,128)S(1)}, u32[]{:S(2)}, u32[]{:S(2)}) collective-permute-start(f32[1,32,256]{2,1,0:T(8,128)S(1)} %get-tuple-element.70), channel_id=1, source_target_pairs={{8,0},{16,8},{24,16},{32,24},{40,32},{48,40},{56,48},{64,56},{72,6... | collective-permute-start | bytes 98312 | tf_op jit(solution)/shard_map/ppermute | solution.py:22
  91.6 11.2 %collective-permute-start.18 = (f32[18,1,256]{2,1,0:T(1,128)S(1)}, f32[18,1,256]{2,1,0:T(1,128)S(1)}, u32[]{:S(2)}, u32[]{:S(2)}) collective-permute-start(f32[18,1,256]{2,1,0:T(1,128)S(1)} %get-tuple-element.45), channel_id=1, source_target_pairs={{0,1},{1,2},{2,3},{3,4},{4,5},{5,6},{6,7},{8,9},{9,10},{10,11},{11... | collective-permute-start | bytes 55304 | tf_op jit(solution)/shard_map/ppermute | solution.py:21
  94.7 8.2 %collective-permute-start.19 = (f32[18,1,256]{2,1,0:T(1,128)S(1)}, f32[18,1,256]{2,1,0:T(1,128)S(1)}, u32[]{:S(2)}, u32[]{:S(2)}) collective-permute-start(f32[18,1,256]{2,1,0:T(1,128)S(1)} %get-tuple-element.46), channel_id=1, source_target_pairs={{1,0},{2,1},{3,2},{4,3},{5,4},{6,5},{7,6},{9,8},{10,9},{11,10},{12... | collective-permute-start | bytes 55304 | tf_op jit(solution)/shard_map/ppermute | solution.py:22
  105.9 12.8 %collective-permute-start.20 = (f32[1,16,128]{2,1,0:T(8,128)S(1)}, f32[1,16,128]{2,1,0:T(8,128)S(1)}, u32[]{:S(2)}, u32[]{:S(2)}) collective-permute-start(f32[1,16,128]{2,1,0:T(8,128)S(1)} %get-tuple-element.93), channel_id=1, source_target_pairs={{0,8},{8,16},{16,24},{24,32},{32,40},{40,48},{48,56},{56,64},{64,7... | collective-permute-start | bytes 24584 | tf_op jit(solution)/shard_map/ppermute | solution.py:21
  110.8 7.9 %collective-permute-start.21 = (f32[1,16,128]{2,1,0:T(8,128)S(1)}, f32[1,16,128]{2,1,0:T(8,128)S(1)}, u32[]{:S(2)}, u32[]{:S(2)}) collective-permute-start(f32[1,16,128]{2,1,0:T(8,128)S(1)} %get-tuple-element.94), channel_id=1, source_target_pairs={{8,0},{16,8},{24,16},{32,24},{40,32},{48,40},{56,48},{64,56},{72,6... | collective-permute-start | bytes 24584 | tf_op jit(solution)/shard_map/ppermute | solution.py:22
  112.8 11.5 %collective-permute-start.14 = (f32[10,1,128]{2,1,0:T(1,128)S(1)}, f32[10,1,128]{2,1,0:T(1,128)S(1)}, u32[]{:S(2)}, u32[]{:S(2)}) collective-permute-start(f32[10,1,128]{2,1,0:T(1,128)S(1)} %get-tuple-element.85), channel_id=1, source_target_pairs={{0,1},{1,2},{2,3},{3,4},{4,5},{5,6},{6,7},{8,9},{9,10},{10,11},{11... | collective-permute-start | bytes 15368 | tf_op jit(solution)/shard_map/ppermute | solution.py:21
  116.7 7.6 %collective-permute-start.15 = (f32[10,1,128]{2,1,0:T(1,128)S(1)}, f32[10,1,128]{2,1,0:T(1,128)S(1)}, u32[]{:S(2)}, u32[]{:S(2)}) collective-permute-start(f32[10,1,128]{2,1,0:T(1,128)S(1)} %get-tuple-element.86), channel_id=1, source_target_pairs={{1,0},{2,1},{3,2},{4,3},{5,4},{6,5},{7,6},{9,8},{10,9},{11,10},{12... | collective-permute-start | bytes 15368 | tf_op jit(solution)/shard_map/ppermute | solution.py:22
  118.7 6.3 %collective-permute-start.22 = (f32[10,1,128]{2,1,0:T(1,128)S(1)}, f32[10,1,128]{2,1,0:T(1,128)S(1)}, u32[]{:S(2)}, u32[]{:S(2)}) collective-permute-start(f32[10,1,128]{2,1,0:T(1,128)S(1)} %get-tuple-element.83), channel_id=1, source_target_pairs={{0,1},{1,2},{2,3},{3,4},{4,5},{5,6},{6,7},{8,9},{9,10},{10,11},{11... | collective-permute-start | bytes 15368 | tf_op jit(solution)/shard_map/ppermute | solution.py:21
  128.7 5.6 collective-permute-start.24
  137.7 5.4 collective-permute-start.26
  150.2 5.0 collective-permute-start.28
  158.7 5.4 collective-permute-start.30
  162.0 5.1 collective-permute-start.31
  170.4 6.0 %collective-permute-start.32 = (f32[1,32,256]{2,1,0:T(8,128)S(1)}, f32[1,32,256]{2,1,0:T(8,128)S(1)}, u32[]{:S(2)}, u32[]{:S(2)}) collective-permute-start(f32[1,32,256]{2,1,0:T(8,128)S(1)} %get-tuple-element.65), channel_id=1, source_target_pairs={{0,8},{8,16},{16,24},{24,32},{32,40},{40,48},{48,56},{56,64},{64,7... | collective-permute-start | bytes 98312 | tf_op jit(solution)/shard_map/ppermute | solution.py:21
  175.0 4.9 collective-permute-start.33
  180.0 5.0 collective-permute-start.34
  183.1 5.1 collective-permute-start.35
  191.6 5.0 collective-permute-start.36
  195.3 4.9 collective-permute-start.37
  200.3 5.0 collective-permute-start.38
  203.4 5.1 collective-permute-start.39
  303.3 6.6 %collective-permute-start.42 = (f32[18,1,256]{2,1,0:T(1,128)S(1)}, f32[18,1,256]{2,1,0:T(1,128)S(1)}, u32[]{:S(2)}, u32[]{:S(2)}) collective-permute-start(f32[18,1,256]{2,1,0:T(1,128)S(1)} %get-tuple-element.37), channel_id=1, source_target_pairs={{0,1},{1,2},{2,3},{3,4},{4,5},{5,6},{6,7},{8,9},{9,10},{10,11},{11... | collective-permute-start | bytes 55304 | tf_op jit(solution)/shard_map/ppermute | solution.py:21
  307.5 5.1 collective-permute-start.43
  323.4 5.3 collective-permute-start.46
  326.7 5.1 collective-permute-start.47
  334.9 5.6 collective-permute-start.48
  343.6 5.2 collective-permute-start.50
  361.0 5.3 collective-permute-start.54
  384.0 5.5 collective-permute-start.58
  387.3 5.1 collective-permute-start.59
  403.7 5.3 collective-permute-start.62
  407.1 5.1 collective-permute-start.63
  504.3 5.9 collective-permute-start.66
  508.3 5.1 collective-permute-start.67
  (94 other events, 1397.5 us)
where the time goes:
time: 607 us; the launch traced here: 596 us
  blocking collectives  240 us (40%)
  starting transfers between devices  178 us (29%)
  waiting for transfers between devices  86.9 us (14%)
  matrix products  29.7 us (5%)
  other arithmetic  27.2 us (4%)
  local copies, waits for them, and re-layouts  25.6 us (4%)
  between operations  8.11 us (1%)
    psum x2, blocking collectives, per_device(): rz_now = lax.psum(jnp.sum(residual * precond * weight_inv), ('gx', 'gy'))  162 us
    ppermute x34, starting transfers between devices, with_halo(): before = lax.ppermute(last, axis, up)  123 us
    ppermute x34, waiting for transfers between devices, with_halo(): after = lax.ppermute(first, axis, down)  86.8 us
    psum x1, blocking collectives, per_device(): curvature = lax.psum(jnp.sum(direction * image * weight_inv), ('gx', 'gy'))  77.4 us
    ppermute x34, starting transfers between devices, with_halo(): after = lax.ppermute(first, axis, down)  55.6 us
  transfers between devices with their start and end apart: 68, of which 27 were waited for; matrix products, arithmetic and copies ran while one was open for 6% of the time, Pallas kernels for 0%

commit v1 on v0

v1 whole, which is shorter than its diff:
```python
import functools
import math

import jax
import jax.numpy as jnp
import numpy as np
from jax import lax
from jax.experimental import pallas as pl
from jax.experimental.pallas import tpu as pltpu
from jax.sharding import PartitionSpec as P

ORDER = 7
COARSE_ORDER = 3
F32 = jnp.float32
BF16 = jnp.bfloat16
MESH = pl.DeviceIdType.MESH

EX, EY, EZ = 2, 4, 32
N, NC = ORDER + 1, COARSE_ORDER + 1
YF, ZF = EY * N, EZ * N
YC, ZC = EY * NC, EZ * NC
ROWS = N * YF
ROWS_C = NC * YC


def legendre_pair(degree, points):
    before = points * 0.0 + 1.0
    now = points.copy()
    for power in range(2, degree + 1):
        after = ((2 * power - 1) * points * now - (power - 1) * before) / power
        before = now
        now = after
    return (now, before)


def gll_tables(degree):
    number = degree + 1
    points = np.cos(math.pi * np.arange(number) / degree)
    for newton in range(60):
        top, below = legendre_pair(degree, points)
        points = points - (points * top - below) / (number * top)
    points = points[::-1].copy()
    points[0] = -1.0
    points[degree] = 1.0
    values = legendre_pair(degree, points)[0]
    weights = 2.0 / (degree * (degree + 1) * values**2)
    derivative = np.zeros((number, number))
    for row_index in range(number):
        for column_index in range(number):
            if row_index != column_index:
                derivative[row_index, column_index] = values[row_index] / (
                    values[column_index] * (points[row_index] - points[column_index])
                )
    derivative[0, 0] = -degree * (degree + 1) / 4.0
    derivative[degree, degree] = degree * (degree + 1) / 4.0
    stiffness = derivative.T @ (weights[:, None] * derivative)
    return (points, weights, stiffness)


def upper_bound(degree):
    points, weights, stiffness = gll_tables(degree)
    rowsum = np.abs(stiffness).sum(1)
    diagonal = np.diag(stiffness)
    outer = lambda a, b, c: a[:, None, None] * b[None, :, None] * c[None, None, :]
    top = outer(rowsum, weights, weights) + outer(weights, rowsum, weights) + outer(weights, weights, rowsum)
    bottom = outer(diagonal, weights, weights) + outer(weights, diagonal, weights) + outer(weights, weights, diagonal)
    return float((top / bottom).max())


def interpolation_matrix(fine_degree, coarse_degree):
    fine_points = gll_tables(fine_degree)[0]
    coarse_points = gll_tables(coarse_degree)[0]
    matrix = np.ones((fine_degree + 1, coarse_degree + 1))
    for column_index in range(coarse_degree + 1):
        for other_index in range(coarse_degree + 1):
            if other_index != column_index:
                matrix[:, column_index] *= (fine_points - coarse_points[other_index]) / (
                    coarse_points[column_index] - coarse_points[other_index]
                )
    return matrix


def cheb_numbers(degree):
    upper = upper_bound(degree)
    lower = 0.1 * upper
    center = 0.5 * (upper + lower)
    half = 0.5 * (upper - lower)
    previous = half / center
    current = 1.0 / (2.0 * center / half - previous)
    k = 2.0 * current / half
    return (1.0 / center, (1.0 + current * previous) / center + k, k)


def sum_matrix(elements, number):
    matrix = np.eye(elements * number)
    for e in range(elements - 1):
        a, b = e * number + number - 1, (e + 1) * number
        matrix[a, b] = matrix[b, a] = 1.0
    return matrix


def blocks(count, matrix):
    return np.kron(np.eye(count), matrix)


TERMS = ((0, 0), (1, 0), (0, 1), (2, 0), (0, 2), (1, 1))
HOW = dict(a=3, b=3, s=6, c=3, d=6, e=3, f=6, g=3)


def pieces_of(matrix, count):
    rest, out = np.asarray(matrix, np.float64), []
    for _ in range(count):
        out.append(rest.astype(np.float32).astype(BF16))
        rest = rest - out[-1].astype(np.float64)
    return out


def right3(matrix, steps="asef"):
    p = pieces_of(matrix, 3)
    return np.concatenate([p[j] for _, j in TERMS[: max(HOW[t] for t in steps)]], 0)


def left3(matrix, steps="asef"):
    p = pieces_of(matrix, 3)
    return np.concatenate([p[j] for _, j in TERMS[: max(HOW[t] for t in steps)]], 1)


def level_matrices(degree):
    _, w, K = gll_tables(degree)
    n = degree + 1
    wy = np.tile(w, EY)
    M0 = np.kron(K, np.diag(wy)) + np.kron(np.diag(w), blocks(EY, K))
    N0 = np.kron(np.diag(w), np.diag(wy))
    return M0, N0, np.diag(np.tile(w, EZ)), blocks(EZ, K)


def face_rows(n):
    y = EY * n
    x = EX * n
    rows = [j for j in range(y)] + [(x - 1) * y + j for j in range(y)]
    rows += [i * y for i in range(x)] + [i * y + y - 1 for i in range(x)]
    return np.array(rows)


@functools.cache
def constants():
    J = interpolation_matrix(ORDER, COARSE_ORDER)
    out = {}
    M0, N0, Wz, Kz = level_matrices(ORDER)
    Sz, Szc = sum_matrix(EZ, N), sum_matrix(EZ, NC)
    Sxy = np.kron(sum_matrix(EX, N), sum_matrix(EY, N))
    Sxyc = np.kron(sum_matrix(EX, NC), sum_matrix(EY, NC))
    Mf, Nf = blocks(EX, M0), blocks(EX, N0)
    SM, SN = Sxy @ Mf, Sxy @ Nf
    F = face_rows(N)
    FC = face_rows(NC)
    out["Bf"] = right3(np.concatenate([Wz @ Sz, Kz @ Sz], 1))
    Sy = np.kron(np.eye(EX * N), sum_matrix(EY, N))
    for e in range(EX):
        cols = slice(e * ROWS, (e + 1) * ROWS)
        full = np.concatenate([(Sy @ Mf)[cols, cols], (Sy @ Nf)[cols, cols]], 1)
        xf = F[e * YF : (e + 1) * YF]
        face = np.concatenate([xf, F[2 * YF :]])
        packed = np.concatenate([SM[face][:, cols], SN[face][:, cols]], 1)
        out[f"Gb{e}"] = left3(np.concatenate([full, packed], 0))
    out["F2F"] = left3(np.concatenate([SM[F][:, F], SN[F][:, F]], 1))
    for e in range(EX):
        rows = slice(e * ROWS, (e + 1) * ROWS)
        here = np.concatenate([np.arange(e * YF, (e + 1) * YF), np.arange(2 * YF, len(F))])
        keep = ((F[here] // ROWS) == e).astype(float)[None, :]
        full = np.concatenate([(Sy @ Mf)[rows][:, F[here]] * keep, (Sy @ Nf)[rows][:, F[here]] * keep], 1)
        out[f"F2A{e}"] = left3(full)
    Rxy = blocks(EX, np.kron(J.T, blocks(EY, J.T)))
    JZ = blocks(EZ, J)
    selc = np.concatenate([np.arange(EX * ROWS_C), FC])
    RM, RN = (Sxyc @ Rxy @ Mf)[selc], (Sxyc @ Rxy @ Nf)[selc]
    out["Br"] = right3(np.concatenate([Wz @ JZ @ Szc, Kz @ JZ @ Szc], 1), "b")
    for e in range(EX):
        cols = slice(e * ROWS, (e + 1) * ROWS)
        out[f"Gr{e}"] = left3(np.concatenate([RM[:, cols], RN[:, cols]], 1), "b")
    out["F2R"] = left3(np.concatenate([RM[:, F], RN[:, F]], 1), "b")
    inv = lambda count: np.where((np.arange(count) % N == 0) | (np.arange(count) % N == N - 1), 0.5, 1.0)
    Wxy = np.kron(np.diag(inv(EX * N)), np.diag(inv(YF)))
    RW = (Sxyc @ Rxy @ Wxy)[selc]
    out["Bw"] = right3(np.diag(inv(ZF)) @ JZ @ Szc, "b")
    out["Gw"] = left3(RW, "b")
    M0c, N0c, Wzc, Kzc = level_matrices(COARSE_ORDER)
    Mc, Nc = blocks(EX, M0c), blocks(EX, N0c)
    out["Bc"] = right3(np.concatenate([Wzc @ Szc, Kzc @ Szc], 1), "c")
    out["Gc"] = left3(np.concatenate([(Sxyc @ Mc)[selc], (Sxyc @ Nc)[selc]], 1), "c")
    Jxy = blocks(EX, np.kron(J, blocks(EY, J)))
    out["Bj"] = right3(np.concatenate([JZ.T @ Wz @ Sz, JZ.T @ Kz @ Sz, JZ.T], 1), "d")
    sel = np.concatenate([np.arange(EX * ROWS), F])
    JM, JN = (SM @ Jxy)[sel], (SN @ Jxy)[sel]
    out["Gj"] = left3(np.concatenate([JM, JN], 1), "d")
    out["Gp"] = left3(Jxy, "d")
    for name, degree, rows in (("f", ORDER, F), ("c", COARSE_ORDER, None)):
        n = degree + 1
        _, w, K = gll_tables(degree)
        kd = np.diag(K)
        S = sum_matrix(EZ, n)
        spread_w = np.zeros((128, EZ * n))
        spread_k = np.zeros((128, EZ * n))
        for ez in range(EZ):
            spread_w[ez, ez * n : (ez + 1) * n] = w
            spread_k[ez, ez * n : (ez + 1) * n] = kd
        out["Bd" + name] = right3(np.concatenate([spread_w @ S, spread_k @ S], 1), "g")
        X, Y = EX * n, EY * n
        left = np.zeros((X * Y, 2, 80))
        for x in range(X):
            for y in range(Y):
                xs = [(x // n, x % n)]
                if x % n == 0:
                    xs.append((x // n - 1, n - 1))
                if x % n == n - 1:
                    xs.append((x // n + 1, 0))
                ys = [(y // n, y % n)]
                if y % n == 0:
                    ys.append((y // n - 1, n - 1))
                if y % n == n - 1:
                    ys.append((y // n + 1, 0))
                for ex, a in xs:
                    for ey, b in ys:
                        dx, dy = ex // EX, ey // EY
                        col = ((dx + 1) * 3 + dy + 1) * 8 + (ex % EX) * EY + ey % EY
                        left[x * Y + y, 0, col] += kd[a] * w[b] + w[a] * kd[b]
                        left[x * Y + y, 1, col] += w[a] * w[b]
        left = left.reshape(X * Y, 160)
        if rows is not None:
            left = np.concatenate([left, left[rows]], 0)
        out["Gd" + name] = left3(left, "g")
    spread = np.zeros((128, ZF + ZC))
    for ez in range(EZ):
        spread[ez, ez * N : (ez + 1) * N] = 1.0
        spread[ez, ZF + ez * NC : ZF + (ez + 1) * NC] = 1.0
    out["Bs"] = np.concatenate([spread.astype(np.float32).astype(BF16)] * 3, 0)
    return out


def dot(a, b):
    return jnp.dot(a, b, preferred_element_type=F32)


def split(x, n):
    out = []
    for i in range(1 + max(i for i, _ in TERMS[:n])):
        out.append(x.astype(BF16))
        x = x - out[-1].astype(F32)
    return out


def rmul(x, b, n, cols=slice(None)):
    p = split(x, n)
    x3 = jnp.concatenate([p[i] for i, _ in TERMS[:n]], 1)
    return dot(x3, b[: x3.shape[1], cols])


def lmul(g, *parts, n, rows=slice(None)):
    split_parts = [split(x, n) for x in parts]
    x3 = jnp.concatenate([p[i] for i, _ in TERMS[:n] for p in split_parts], 0)
    return dot(g[rows, : x3.shape[0]], x3)


def kernel_body(shape, names, rhs_ref, coef_ref, *refs):
    gxn, gyn, nz = shape
    ny = gxn // nz
    n_const = len(names)
    const_hbm = dict(zip(names, refs[:n_const]))
    sol_ref, res_ref = refs[n_const : n_const + 2]
    rest = refs[n_const + 2 :]
    const = dict(zip(names, rest[:n_const]))
    (Fr, Zr, Dr, Cr, DFr, DcFr, Lr, Sr, Rr, Ar, FXr, Wr, WLr,
     Dc_r, Cc_r, g_r, e_r, cpad, tiles,
     sx, sy, rx, ry, rc, csx, csy, crx, cry, crc, dots, dred,
     const_sem, send_sem, recv_sem, csend_sem, crecv_sem, tsend_sem, trecv_sem, dsend_sem, drecv_sem) = rest[n_const:]

    inv_center, a_f, k_f = cheb_numbers(ORDER)
    inv_center_c, a_c, k_c = cheb_numbers(COARSE_ORDER)
    px, py = lax.axis_index("gx"), lax.axis_index("gy")

    def at(dx, dy):
        return (lax.rem(px + dx + gxn, gxn), lax.rem(py + dy + gyn, gyn))

    around = [(dx, dy) for dx in (-1, 0, 1) for dy in (-1, 0, 1) if (dx, dy) != (0, 0)]
    pz, pyy = lax.rem(px, nz), px // nz
    stages = [
        [(px, lax.rem(py + d, gyn)) for d in range(1, gyn)],
        [(pyy * nz + lax.rem(pz + d, nz), py) for d in range(1, nz)],
        [(lax.rem(pyy + d, ny) * nz + pz, py) for d in range(1, ny)],
    ]

    copies = [pltpu.make_async_copy(const_hbm[m], const[m], const_sem.at[i]) for i, m in enumerate(names)]
    for c in copies:
        c.start()

    rc[...] = jnp.zeros_like(rc)
    crc[...] = jnp.zeros_like(crc)
    tiles[...] = jnp.zeros_like(tiles)
    cpad[...] = jnp.zeros_like(cpad)
    cpad[0:EY, 0:EZ] = coef_ref[0]
    cpad[EY : 2 * EY, 0:EZ] = coef_ref[1]

    barrier = pltpu.get_barrier_semaphore()
    partners = [at(dx, dy) for dx, dy in around] + [p for st in stages for p in st]
    for p in partners:
        pl.semaphore_signal(barrier, inc=1, device_id=p, device_id_type=MESH)

    def local_sum(v):
        rows = lax.broadcasted_iota(jnp.int32, v.shape, 0)
        lanes = lax.broadcasted_iota(jnp.int32, v.shape, 1)
        y = lax.rem(rows, YF)
        up = (lax.rem(y, N) == N - 1) & (y != YF - 1)
        down = (lax.rem(y, N) == 0) & (y != 0)
        v = v + jnp.where(up, pltpu.roll(v, ROWS - 1, 0), 0.0) + jnp.where(down, pltpu.roll(v, 1, 0), 0.0)
        up = (lax.rem(lanes, N) == N - 1) & (lanes != ZF - 1)
        down = (lax.rem(lanes, N) == 0) & (lanes != 0)
        return v + jnp.where(up, pltpu.roll(v, ZF - 1, 1), 0.0) + jnp.where(down, pltpu.roll(v, 1, 1), 0.0)

    def middle(ref, *index):
        total = ref[(*index, 0, pl.ds(ROWS - YF, YF))] + ref[(*index, 1, pl.ds(0, YF))]
        ref[(*index, 0, pl.ds(ROWS - YF, YF))] = total
        ref[(*index, 1, pl.ds(0, YF))] = total

    for e in range(EX):
        Fr[0, e] = local_sum(rhs_ref[e])
    middle(Fr, 0)
    sx[0, 0] = Fr[0, 0, 0:YF]
    sx[0, 1] = Fr[0, 1, ROWS - YF : ROWS]
    for x in range(EX * N):
        e, r = x // N, (x % N) * YF
        sy[0, 0, x : x + 1] = Fr[0, e, r : r + 1]
        sy[0, 1, x : x + 1] = Fr[0, e, r + YF - 1 : r + YF]

    def exchange(i, sx, sy, rx, ry, rc, send_sem, recv_sem):
        last = sy.shape[2] - 1
        plan = [
            (sx.at[i, 0], rx.at[i, 1], at(-1, 0)),
            (sx.at[i, 1], rx.at[i, 0], at(1, 0)),
            (sy.at[i, 0], ry.at[i, 1], at(0, -1)),
            (sy.at[i, 1], ry.at[i, 0], at(0, 1)),
            (sy.at[i, 0, pl.ds(0, 1)], rc.at[i, 1, pl.ds(last, 1)], at(-1, -1)),
            (sy.at[i, 0, pl.ds(last, 1)], rc.at[i, 1, pl.ds(0, 1)], at(1, -1)),
            (sy.at[i, 1, pl.ds(0, 1)], rc.at[i, 0, pl.ds(last, 1)], at(-1, 1)),
            (sy.at[i, 1, pl.ds(last, 1)], rc.at[i, 0, pl.ds(0, 1)], at(1, 1)),
        ]
        return [
            pltpu.make_async_remote_copy(
                src_ref=s, dst_ref=d, send_sem=send_sem.at[i, j], recv_sem=recv_sem.at[i, j],
                device_id=dev, device_id_type=MESH,
            )
            for j, (s, d, dev) in enumerate(plan)
        ]

    def fine(i):
        return exchange(i, sx, sy, rx, ry, rc, send_sem, recv_sem)

    def coarse(i):
        return exchange(i, csx, csy, crx, cry, crc, csend_sem, crecv_sem)

    def start(copies):
        for c in copies:
            c.start()

    def arrive(copies):
        for c in copies:
            c.wait_recv()

    pl.semaphore_wait(barrier, len(partners))

    tile_copies = []
    for j, (dx, dy) in enumerate(around):
        slot = ((1 - dx) * 3 + (1 - dy)) * 8
        tile_copies.append(pltpu.make_async_remote_copy(
            src_ref=cpad, dst_ref=tiles.at[pl.ds(slot, 8)], send_sem=tsend_sem.at[j], recv_sem=trecv_sem.at[j],
            device_id=at(dx, dy), device_id_type=MESH,
        ))
    start(tile_copies)
    start(fine(0))
    tiles[32:40] = cpad[...]

    for c in copies:
        c.wait()
    own = cpad[...]
    h1 = own.astype(BF16)
    r1 = own - h1.astype(F32)
    h2 = r1.astype(BF16)
    h3 = (r1 - h2.astype(F32)).astype(BF16)
    spread = dot(jnp.concatenate([h1, h2, h3], 1), const["Bs"][...])
    for e in range(EX):
        lines = [spread[e * EY + ey : e * EY + ey + 1] for ey in range(EY)]
        cf = [jnp.broadcast_to(l[:, :ZF], (N, ZF)) for l in lines]
        one = jnp.concatenate(cf, 0)
        Cr[e] = jnp.concatenate([one] * N, 0)
        FXr[0, e * YF : (e + 1) * YF] = one
        FXr[0, 2 * YF + e * N : 2 * YF + (e + 1) * N] = cf[0]
        FXr[0, 2 * YF + (EX + e) * N : 2 * YF + (EX + e + 1) * N] = cf[EY - 1]
        cc = jnp.concatenate([jnp.broadcast_to(l[:, ZF:], (NC, ZC)) for l in lines], 0)
        Cc_r[e * ROWS_C : (e + 1) * ROWS_C] = jnp.concatenate([cc] * NC, 0)

    rows = lax.broadcasted_iota(jnp.int32, (ROWS, ZF), 0)
    lanes = lax.broadcasted_iota(jnp.int32, (ROWS, ZF), 1)
    xr, yr = rows // YF, lax.rem(rows, YF)

    def edge(i):
        return (lax.rem(i, N) == 0) | (lax.rem(i, N) == N - 1)

    wz = jnp.where(edge(lanes), 0.5, 1.0)
    Wr[...] = wz * jnp.where(edge(yr), 0.5, 1.0) * jnp.where(edge(xr), 0.5, 1.0)
    wl = wz * jnp.where(edge(yr) & (yr != 0) & (yr != YF - 1), 0.5, 1.0)
    WLr[0] = wl * jnp.where(xr == N - 1, 0.5, 1.0)
    WLr[1] = wl * jnp.where(xr == 0, 0.5, 1.0)

    arrive(tile_copies)
    ext = tiles[...]
    pd = rmul(ext, const["Bdf"], HOW["g"])
    diag = lmul(const["Gdf"], pd[:, :ZF], pd[:, ZF:], n=HOW["g"])

    def mask_of(x, y, z, n):
        inside = (x != 0) & (x != gxn * EX * n - 1) & (y != 0) & (y != gyn * EY * n - 1)
        return inside & (z != 0) & (z != EZ * n - 1)

    for e in range(EX):
        keep = mask_of(px * EX * N + e * N + xr, py * YF + yr, lanes, N)
        Dr[e] = jnp.where(keep, 1.0 / diag[e * ROWS : (e + 1) * ROWS], 0.0)
    frow = lax.broadcasted_iota(jnp.int32, (96, ZF), 0)
    flane = lax.broadcasted_iota(jnp.int32, (96, ZF), 1)
    fx = jnp.where(frow < YF, 0, jnp.where(frow < 2 * YF, EX * N - 1, lax.rem(frow, EX * N)))
    fy = jnp.where(frow < 2 * YF, lax.rem(frow, YF), jnp.where(frow < 2 * YF + EX * N, 0, YF - 1))
    keep = mask_of(px * EX * N + fx, py * YF + fy, flane, N)
    df = jnp.where(keep, 1.0 / diag[EX * ROWS :], 0.0)
    DFr[...] = df
    DcFr[...] = df * FXr[0]
    pdc = rmul(ext, const["Bdc"], HOW["g"])
    diag_c = lmul(const["Gdc"], pdc[:, :ZC], pdc[:, ZC:], n=HOW["g"])
    crow = lax.broadcasted_iota(jnp.int32, (EX * ROWS_C, ZC), 0)
    clane = lax.broadcasted_iota(jnp.int32, (EX * ROWS_C, ZC), 1)
    keep = mask_of(px * EX * NC + crow // YC, py * YC + lax.rem(crow, YC), clane, NC)
    Dc_r[...] = jnp.where(keep, 1.0 / diag_c, 0.0)

    def halo(i):
        arrive(fine(i))
        return jnp.concatenate([rx[i, 0], rx[i, 1], ry[i, 0] + rc[i, 0], ry[i, 1] + rc[i, 1]], 0)

    def add_faces(ref, index, h):
        ref[(*index, 0, pl.ds(0, YF))] += h[0:YF]
        ref[(*index, 1, pl.ds(ROWS - YF, YF))] += h[YF : 2 * YF]
        for x in range(EX * N):
            e, r = x // N, (x % N) * YF
            ref[(*index, e, pl.ds(r, 1))] += h[2 * YF + x : 2 * YF + x + 1]
            b = 2 * YF + EX * N + x
            ref[(*index, e, pl.ds(r + YF - 1, 1))] += h[b : b + 1]

    def bulk(values, n):
        y0 = y1 = None
        for e in range(EX):
            p = rmul(values(e), const["Bf"], n)
            o = lmul(const[f"Gb{e}"], p[:, :ZF], p[:, ZF:], n=n)
            Lr[e] = o[:ROWS]
            FXr[1, e * YF : (e + 1) * YF] = o[ROWS : ROWS + YF]
            y0 = o[ROWS + YF :] if e == 0 else y0 + o[ROWS + YF :]
        FXr[1, 2 * YF :] = y0

    def face_z(hs, n):
        return rmul(hs, const["Bf"], n)

    def send_faces(i, faces):
        sx[i, 0] = faces[0:YF]
        sx[i, 1] = faces[YF : 2 * YF]
        sy[i, 0] = faces[2 * YF : 2 * YF + EX * N]
        sy[i, 1] = faces[2 * YF + EX * N :]
        start(fine(i))

    def face_to_face(ph, n):
        return lmul(const["F2F"], ph[:, :ZF], ph[:, ZF:], n=n)

    def face_to_all(ph, n):
        for e in range(EX):
            part = jnp.concatenate([ph[e * YF : (e + 1) * YF], ph[2 * YF :]], 0)
            Lr[e] += lmul(const[f"F2A{e}"], part[:, :ZF], part[:, ZF:], n=n)
        middle(Lr)

    def coarse_faces(i, o):
        csx[i, 0] = o[0:YC]
        csx[i, 1] = o[YC : 2 * YC]
        csy[i, 0] = o[2 * YC : 2 * YC + EX * NC]
        csy[i, 1] = o[2 * YC + EX * NC :]
        start(coarse(i))

    def coarse_arrive(i, ref):
        arrive(coarse(i))
        ref[0:YC] += crx[i, 0]
        ref[EX * ROWS_C - YC : EX * ROWS_C] += crx[i, 1]
        h0, h1 = cry[i, 0] + crc[i, 0], cry[i, 1] + crc[i, 1]
        for x in range(EX * NC):
            ref[x * YC : x * YC + 1] += h0[x : x + 1]
            ref[x * YC + YC - 1 : x * YC + YC] += h1[x : x + 1]

    def cycle(k, carry):
        bulk(lambda e: Cr[e] * (Dr[e] * inv_center) * Fr[k, e], HOW["a"])
        h = halo(4 * k)
        ph = face_z(DcFr[...] * inv_center * h, HOW["a"])
        send_faces(4 * k + 1, FXr[1] + face_to_face(ph, HOW["a"]))
        add_faces(Fr, (k,), h)
        face_to_all(ph, HOW["a"])
        gl = None
        for e in range(EX):
            s = Dr[e] * (a_f * Fr[k, e] - k_f * Lr[e])
            Sr[e] = s
            p = rmul(Cr[e] * s, const["Br"], HOW["b"])
            f = rmul(Fr[k, e], const["Bw"], HOW["b"])
            o = -lmul(const[f"Gr{e}"], p[:, :ZC], p[:, ZC:], n=HOW["b"])
            gl = o if e == 0 else gl + o
            Ar[e, :, 0:ZC] = f
        gl = gl + lmul(const["Gw"], Ar[0, :, 0:ZC], Ar[1, :, 0:ZC], n=HOW["b"])
        h = halo(4 * k + 1)
        hs = (-k_f) * DcFr[...] * h
        pr = rmul(hs, const["Br"], HOW["b"])
        gl = gl - lmul(const["F2R"], pr[:, :ZC], pr[:, ZC:], n=HOW["b"])
        coarse_faces(2 * k, gl[EX * ROWS_C :])
        g_r[...] = gl[: EX * ROWS_C]
        bulk(lambda e: Cr[e] * Sr[e], HOW["s"])
        ph = face_z(hs, HOW["s"])
        face_to_all(ph, HOW["s"])
        FXr[1] = FXr[1] + face_to_face(ph, HOW["s"])
        add_faces(Sr, (), (-k_f) * DFr[...] * h)
        coarse_arrive(2 * k, g_r)
        p = rmul(Cc_r[...] * (Dc_r[...] * inv_center_c) * g_r[...], const["Bc"], HOW["c"])
        o = lmul(const["Gc"], p[:, :ZC], p[:, ZC:], n=HOW["c"])
        coarse_faces(2 * k + 1, o[EX * ROWS_C :])
        e_r[...] = o[: EX * ROWS_C]
        coarse_arrive(2 * k + 1, e_r)
        fix = Dc_r[...] * (a_c * g_r[...] - k_c * e_r[...])
        p = rmul(Cc_r[...] * fix, const["Bj"], HOW["d"], slice(0, 2 * ZF))
        o = lmul(const["Gj"], p[:, :ZF], p[:, ZF:], n=HOW["d"])
        send_faces(4 * k + 2, FXr[1] + o[EX * ROWS :])
        p = rmul(fix, const["Bj"], HOW["d"], slice(2 * ZF, 3 * ZF))
        up = lmul(const["Gp"], p, n=HOW["d"])
        for e in range(EX):
            rows = slice(e * ROWS, (e + 1) * ROWS)
            Sr[e] = Sr[e] + up[rows]
            Rr[e] = Fr[k, e] - Lr[e] - o[rows]
        bulk(lambda e: Cr[e] * (Dr[e] * inv_center) * Rr[e], HOW["e"])
        h = halo(4 * k + 2)
        ph = face_z((-inv_center) * DcFr[...] * h, HOW["e"])
        send_faces(4 * k + 3, FXr[1] + face_to_face(ph, HOW["e"]))
        add_faces(Rr, (), -h)
        face_to_all(ph, HOW["e"])
        for e in range(EX):
            Zr[k, e] = Sr[e] + Dr[e] * (a_f * Rr[e] - k_f * Lr[e])
        bulk(lambda e: Cr[e] * Zr[k, e], HOW["f"])
        h = halo(4 * k + 3)
        ph = face_z((-k_f) * DcFr[...] * h, HOW["f"])
        send_faces(4 * k + 4, FXr[1] + face_to_face(ph, HOW["f"]))
        add_faces(Zr, (k,), (-k_f) * DFr[...] * h)
        face_to_all(ph, HOW["f"])
        sums = [0.0] * 4
        for e in range(EX):
            z, l = Zr[k, e], Lr[e]
            Fr[k + 1, e] = l
            wz = Wr[...] * z
            wl = WLr[e] * l
            for i, t in enumerate((Fr[0, e] * wz, Fr[k, e] * wz, Zr[0, e] * wl, z * wl)):
                t = jnp.sum(t, axis=0, keepdims=True)
                sums[i] = sums[i] + t[:, : ZF // 2] + t[:, ZF // 2 :]
        dots[k, 0:4] = jnp.concatenate(sums, 0)
        return carry

    lax.fori_loop(0, 2, cycle, 0)

    dred[0, 0, 0:4] = dots[0, 0:4]
    dred[0, 0, 4:8] = dots[1, 0:4]
    dot_copies = []
    count = 0
    for s, stage in enumerate(stages):
        now = []
        for j, p in enumerate(stage):
            now.append(pltpu.make_async_remote_copy(
                src_ref=dred.at[s, 0], dst_ref=dred.at[s, j + 1], send_sem=dsend_sem.at[count], recv_sem=drecv_sem.at[count],
                device_id=p, device_id_type=MESH,
            ))
            count += 1
        start(now)
        arrive(now)
        total = dred[s, 0]
        for j in range(len(stage)):
            total = total + dred[s, j + 1]
        dred[s + 1, 0] = total
        dot_copies += now
    lanes_sum = jnp.sum(dred[3, 0], axis=1, keepdims=True)
    pick = lambda i: lanes_sum[i : i + 1, 0:1]
    rz0, c00 = pick(1), pick(3)
    r0u, wu, zv, uv = pick(4), pick(5), pick(6), pick(7)
    alpha0 = rz0 / c00
    rz1 = alpha0 * (alpha0 * wu - r0u)
    beta1 = 1.0 + rz1 / rz0
    curve = beta1 * beta1 * c00 - beta1 * alpha0 * (zv + wu) + alpha0 * alpha0 * uv
    alpha1 = rz1 / curve
    c_z = alpha0 + alpha1 * beta1
    c_u = alpha1 * alpha0
    for e in range(EX):
        sol_ref[e] = c_z * Zr[0, e] - c_u * Zr[1, e]
    h = halo(8)
    add_faces(Fr, (2,), h)
    for e in range(EX):
        res_ref[e] = jnp.where(Dr[e] > 0.0, Fr[0, e] - c_z * Fr[1, e] + c_u * Fr[2, e], 0.0)

    for c in tile_copies + dot_copies:
        c.wait_send()

    def drain(i, carry):
        for c in fine(i):
            c.wait_send()
        return carry

    lax.fori_loop(0, 9, drain, 0)

    def drain_c(i, carry):
        for c in coarse(i):
            c.wait_send()
        return carry

    lax.fori_loop(0, 4, drain_c, 0)


def solution(mesh):
    gxn, gyn = mesh.shape["gx"], mesh.shape["gy"]
    nz = 8 if gxn == 32 else 2
    ny = gxn // nz
    table = constants()
    names = tuple(table)
    n_dots = gyn - 1 + nz - 1 + ny - 1
    most = max(gyn, nz, ny)

    def per_device(right_side, coefficient):
        rhs = right_side.reshape(EX, ROWS, ZF)
        field = (EX, ROWS, ZF)
        vm = lambda *s: pltpu.VMEM(s, F32)
        dma = lambda *s: pltpu.SemaphoreType.DMA(s)
        scratch = [pltpu.VMEM(table[m].shape, BF16) for m in names]
        scratch += [
            vm(3, *field), vm(2, *field), vm(*field), vm(*field), vm(96, ZF), vm(96, ZF),
            vm(*field), vm(*field), vm(*field), vm(*field), vm(2, 96, ZF), vm(ROWS, ZF), vm(*field),
            vm(EX * ROWS_C, ZC), vm(EX * ROWS_C, ZC), vm(EX * ROWS_C, ZC), vm(EX * ROWS_C, ZC), vm(8, 128), vm(80, 128),
            vm(9, 2, YF, ZF), vm(9, 2, EX * N, ZF), vm(9, 2, YF, ZF), vm(9, 2, EX * N, ZF), vm(9, 2, EX * N, ZF),
            vm(4, 2, YC, ZC), vm(4, 2, EX * NC, ZC), vm(4, 2, YC, ZC), vm(4, 2, EX * NC, ZC), vm(4, 2, EX * NC, ZC),
            vm(2, 8, 128), vm(4, most, 8, 128),
            dma(len(names)), dma(9, 8), dma(9, 8), dma(4, 8), dma(4, 8), dma(8), dma(8), dma(n_dots), dma(n_dots),
        ]
        sol, res = pl.pallas_call(
            functools.partial(kernel_body, (gxn, gyn, nz), names),
            out_shape=[jax.ShapeDtypeStruct(field, F32)] * 2,
            in_specs=[pl.BlockSpec(memory_space=pltpu.VMEM)] * 2 + [pl.BlockSpec(memory_space=pl.ANY)] * len(names),
            out_specs=[pl.BlockSpec(memory_space=pltpu.VMEM)] * 2,
            scratch_shapes=scratch,
            compiler_params=pltpu.CompilerParams(
                collective_id=0, has_side_effects=True, vmem_limit_bytes=56 * 2**20
            ),
        )(rhs, coefficient, *[jnp.asarray(table[m]) for m in names])
        return sol.reshape(right_side.shape), res.reshape(right_side.shape)

    spec = P("gx", "gy", None)
    return jax.shard_map(
        per_device, mesh=mesh, in_specs=(spec, spec), out_specs=(spec, spec), check_vma=False
    )
```

time: 607 us -> 100 us (0.16); the launches traced: 596 us -> 100 us
  blocking collectives: 240 us -> 0 us
  starting transfers between devices: 178 us -> 0 us
  Pallas kernels: 0 us -> 95.7 us
  waiting for transfers between devices: 86.9 us -> 0 us
  matrix products: 29.7 us -> 0 us
  other arithmetic: 27.2 us -> 0 us
  local copies, waits for them, and re-layouts: 25.6 us -> 3.76 us
  between operations: 8.11 us -> 0.64 us
    psum x3 -> x0, blocking collectives: 240 us -> none  [the longest x2 162 us: per_device(): rz_now = lax.psum(jnp.sum(residual * precond * weight_inv), ('gx', 'gy'))]
    ppermute x68 -> x0, starting transfers between devices: 178 us -> none  [the longest x34 123 us: with_halo(): before = lax.ppermute(last, axis, up)]
    pallas_call x0 -> x1, Pallas kernels: none -> 95.7 us  [per_device(): pl.pallas_call(functools.partial(kernel_body, (gxn, gyn, nz), names), out...]
    ppermute x68 -> x0, waiting for transfers between devices: 86.9 us -> none  [the longest x34 86.8 us: with_halo(): after = lax.ppermute(first, axis, down)]
    dot_general x48 -> x0, matrix products: 29.7 us -> none  [the longest x16 11.7 us: along_first(): jnp.einsum('ai,xiyz->xayz', matrix, shaped, precision=lax.Precision.HIGHEST)]
    another operation x16 -> x0, local copies, waits for them, and re-layouts: 9.58 us -> none  [the longest x6 3.95 us: build_level(): jnp.tile(diagonal, coefficient.shape[dim_index])]
    add x44 -> x0, other arithmetic: 8.75 us -> none  [the longest x15 2.65 us: sum_first(): return padded[1:-1] + upper * padded[2:] + lower * padded[:-2]]
    mul x16 -> x0, local copies, waits for them, and re-layouts: 7.83 us -> none  [the longest x4 6.78 us: along_third(): block = jnp.kron(jnp.eye(group, dtype=jnp.float32), matrix)]
  transfers between devices with their start and end apart: 68 -> 0, of which waited for: 27 -> 0; matrix products, arithmetic and copies ran while one was open for 6% -> 0% of each run, Pallas kernels for 0% -> 0%
where the time goes in v1:
time: 100 us
  Pallas kernels  95.7 us (96%)
  local copies, waits for them, and re-layouts  3.76 us (4%)
    pallas_call x1, Pallas kernels, per_device(): pl.pallas_call(functools.partial(kernel_body, (gxn, gyn, nz), names), out...  95.7 us
    unnamed x2, local copies, waits for them, and re-layouts  3.76 us

profile of v1, /device:TPU:1, one launch (start us, length us, event | category | flops | bytes accessed | tf_op | source)
XLA Modules:
  0.0 100.1 jit_solution(16508205024388712881)
XLA Ops:
  0.6 95.7 %shard_map.239 = (f32[2,256,256]{2,1,0:T(8,128)}, f32[2,256,256]{2,1,0:T(8,128)}) custom-call(f32[2,256,256]{2,1,0:T(8,128)} %bitcast.3, f32[2,4,32]{2,1,0:T(4,128)} %coef_ref.1, bf16[1536,512]{1,0:T(8,128)(2,1)} %constant.44.clone.refs_0_, bf16[320,3072]{1,0:T(8,128)(2,1)} %constant.45.clone.refs_1_, bf16[320,3072]{1,0:T(8,128)(2,1)} %constant.46.clone.refs_2_, ...), custom_call_target="tpu_custom_call" | custom-call | tf_op jit(solution)/shard_map/pallas_call | solution.py:649
  96.3 1.9 %copy.28 = f32[16,32,256]{2,1,0:T(8,128)} copy(f32[16,32,256]{2,1,0:T(8,128)} %bitcast.5) | data formatting | bytes 1048576
  98.2 1.9 %copy.29 = f32[16,32,256]{2,1,0:T(8,128)} copy(f32[16,32,256]{2,1,0:T(8,128)} %bitcast.4) | data formatting | bytes 1048576

commit v2 on v1

v2 whole, which is shorter than its diff:
```python
import functools
import math

import jax
import jax.numpy as jnp
import numpy as np
from jax import lax
from jax.experimental import pallas as pl
from jax.experimental.pallas import tpu as pltpu
from jax.sharding import PartitionSpec as P

ORDER = 7
COARSE_ORDER = 3
F32 = jnp.float32
BF16 = jnp.bfloat16
MESH = pl.DeviceIdType.MESH

EX, EY, EZ = 2, 4, 32
N, NC = ORDER + 1, COARSE_ORDER + 1
YF, ZF = EY * N, EZ * N
YC, ZC = EY * NC, EZ * NC
ROWS = N * YF
ROWS_C = NC * YC


def legendre_pair(degree, points):
    before = points * 0.0 + 1.0
    now = points.copy()
    for power in range(2, degree + 1):
        after = ((2 * power - 1) * points * now - (power - 1) * before) / power
        before = now
        now = after
    return (now, before)


def gll_tables(degree):
    number = degree + 1
    points = np.cos(math.pi * np.arange(number) / degree)
    for newton in range(60):
        top, below = legendre_pair(degree, points)
        points = points - (points * top - below) / (number * top)
    points = points[::-1].copy()
    points[0] = -1.0
    points[degree] = 1.0
    values = legendre_pair(degree, points)[0]
    weights = 2.0 / (degree * (degree + 1) * values**2)
    derivative = np.zeros((number, number))
    for row_index in range(number):
        for column_index in range(number):
            if row_index != column_index:
                derivative[row_index, column_index] = values[row_index] / (
                    values[column_index] * (points[row_index] - points[column_index])
                )
    derivative[0, 0] = -degree * (degree + 1) / 4.0
    derivative[degree, degree] = degree * (degree + 1) / 4.0
    stiffness = derivative.T @ (weights[:, None] * derivative)
    return (points, weights, stiffness)


def upper_bound(degree):
    points, weights, stiffness = gll_tables(degree)
    rowsum = np.abs(stiffness).sum(1)
    diagonal = np.diag(stiffness)
    outer = lambda a, b, c: a[:, None, None] * b[None, :, None] * c[None, None, :]
    top = outer(rowsum, weights, weights) + outer(weights, rowsum, weights) + outer(weights, weights, rowsum)
    bottom = outer(diagonal, weights, weights) + outer(weights, diagonal, weights) + outer(weights, weights, diagonal)
    return float((top / bottom).max())


def interpolation_matrix(fine_degree, coarse_degree):
    fine_points = gll_tables(fine_degree)[0]
    coarse_points = gll_tables(coarse_degree)[0]
    matrix = np.ones((fine_degree + 1, coarse_degree + 1))
    for column_index in range(coarse_degree + 1):
        for other_index in range(coarse_degree + 1):
            if other_index != column_index:
                matrix[:, column_index] *= (fine_points - coarse_points[other_index]) / (
                    coarse_points[column_index] - coarse_points[other_index]
                )
    return matrix


def cheb_numbers(degree):
    upper = upper_bound(degree)
    lower = 0.1 * upper
    center = 0.5 * (upper + lower)
    half = 0.5 * (upper - lower)
    previous = half / center
    current = 1.0 / (2.0 * center / half - previous)
    k = 2.0 * current / half
    return (1.0 / center, (1.0 + current * previous) / center + k, k)


def sum_matrix(elements, number):
    matrix = np.eye(elements * number)
    for e in range(elements - 1):
        a, b = e * number + number - 1, (e + 1) * number
        matrix[a, b] = matrix[b, a] = 1.0
    return matrix


def blocks(count, matrix):
    return np.kron(np.eye(count), matrix)


TERMS = ((0, 0), (1, 0), (0, 1), (2, 0), (0, 2), (1, 1))
HOW = dict(a=3, b=3, s=6, c=3, d=6, e=3, f=6, g=3, h=3)


def pieces_of(matrix, count):
    rest, out = np.asarray(matrix, np.float64), []
    for _ in range(count):
        out.append(rest.astype(np.float32).astype(BF16))
        rest = rest - out[-1].astype(np.float64)
    return out


def right3(matrix, steps="asef"):
    p = pieces_of(matrix, 3)
    return np.concatenate([p[j] for _, j in TERMS[: max(HOW[t] for t in steps)]], 0)


def left3(matrix, steps="asef"):
    p = pieces_of(matrix, 3)
    return np.concatenate([p[j] for _, j in TERMS[: max(HOW[t] for t in steps)]], 1)


def level_matrices(degree):
    _, w, K = gll_tables(degree)
    n = degree + 1
    wy = np.tile(w, EY)
    M0 = np.kron(K, np.diag(wy)) + np.kron(np.diag(w), blocks(EY, K))
    N0 = np.kron(np.diag(w), np.diag(wy))
    return M0, N0, np.diag(np.tile(w, EZ)), blocks(EZ, K)


def face_rows(n):
    y = EY * n
    x = EX * n
    rows = [j for j in range(y)] + [(x - 1) * y + j for j in range(y)]
    rows += [i * y for i in range(x)] + [i * y + y - 1 for i in range(x)]
    return np.array(rows)


def coarse_places():
    XC = EX * NC
    before, after_x, after_y = range(-NC, 0), range(XC, XC + NC), range(YC, YC + NC)
    grids = [(range(XC), range(YC)), (before, range(YC)), (after_x, range(YC)), (range(XC), before), (range(XC), after_y)]
    grids += [(a, b) for a in (before, after_x) for b in (before, after_y)]
    both = [(x, y) for xs, ys in grids for x in xs for y in ys]
    return np.array([p[0] for p in both]), np.array([p[1] for p in both])


@functools.cache
def constants():
    J = interpolation_matrix(ORDER, COARSE_ORDER)
    out = {}
    M0, N0, Wz, Kz = level_matrices(ORDER)
    Sz, Szc = sum_matrix(EZ, N), sum_matrix(EZ, NC)
    Sxy = np.kron(sum_matrix(EX, N), sum_matrix(EY, N))
    Sxyc = np.kron(sum_matrix(EX, NC), sum_matrix(EY, NC))
    Mf, Nf = blocks(EX, M0), blocks(EX, N0)
    SM, SN = Sxy @ Mf, Sxy @ Nf
    F = face_rows(N)
    out["Bf"] = right3(np.concatenate([Wz @ Sz, Kz @ Sz], 1))
    Sy = np.kron(np.eye(EX * N), sum_matrix(EY, N))
    for e in range(EX):
        cols = slice(e * ROWS, (e + 1) * ROWS)
        full = np.concatenate([(Sy @ Mf)[cols, cols], (Sy @ Nf)[cols, cols]], 1)
        xf = F[e * YF : (e + 1) * YF]
        face = np.concatenate([xf, F[2 * YF :]])
        packed = np.concatenate([SM[face][:, cols], SN[face][:, cols]], 1)
        out[f"Gb{e}"] = left3(np.concatenate([full, packed], 0))
    out["F2F"] = left3(np.concatenate([SM[F][:, F], SN[F][:, F]], 1))
    for e in range(EX):
        rows = slice(e * ROWS, (e + 1) * ROWS)
        here = np.concatenate([np.arange(e * YF, (e + 1) * YF), np.arange(2 * YF, len(F))])
        keep = ((F[here] // ROWS) == e).astype(float)[None, :]
        full = np.concatenate([(Sy @ Mf)[rows][:, F[here]] * keep, (Sy @ Nf)[rows][:, F[here]] * keep], 1)
        out[f"F2A{e}"] = left3(full)
    Rxy = blocks(EX, np.kron(J.T, blocks(EY, J.T)))
    JZ = blocks(EZ, J)
    XC = EX * NC
    first = [x * YC + y for x in range(XC) for y in range(NC)]
    last = [x * YC + YC - NC + y for x in range(XC) for y in range(NC)]
    selc = np.concatenate([np.arange(XC * YC), first, last]).astype(int)
    RM, RN = (Sxyc @ Rxy @ Mf)[selc], (Sxyc @ Rxy @ Nf)[selc]
    out["Br"] = right3(np.concatenate([Wz @ JZ @ Szc, Kz @ JZ @ Szc], 1), "b")
    for e in range(EX):
        cols = slice(e * ROWS, (e + 1) * ROWS)
        out[f"Gr{e}"] = left3(np.concatenate([RM[:, cols], RN[:, cols]], 1), "b")
    out["F2R"] = left3(np.concatenate([RM[:, F], RN[:, F]], 1), "b")
    inv = lambda count: np.where((np.arange(count) % N == 0) | (np.arange(count) % N == N - 1), 0.5, 1.0)
    Wxy = np.kron(np.diag(inv(EX * N)), np.diag(inv(YF)))
    RW = (Sxyc @ Rxy @ Wxy)[selc]
    out["Bw"] = right3(np.diag(inv(ZF)) @ JZ @ Szc, "b")
    out["Gw"] = left3(RW, "b")
    _, wc, Kc = gll_tables(COARSE_ORDER)
    Wzc, Kzc = np.diag(np.tile(wc, EZ)), blocks(EZ, Kc)
    out["Bc"] = right3(np.concatenate([Wzc @ Szc, Kzc @ Szc], 1), "c")
    cx, cy = coarse_places()
    grid = (cx + NC) * (YC + 2 * NC) + cy + NC
    wx4, wy6 = np.diag(np.tile(wc, EX + 2)), np.diag(np.tile(wc, EY + 2))
    Me = np.kron(blocks(EX + 2, Kc), wy6) + np.kron(wx4, blocks(EY + 2, Kc))
    Ne = np.kron(wx4, wy6)
    Se = np.kron(sum_matrix(EX + 2, NC), sum_matrix(EY + 2, NC))
    own = grid[: XC * YC]
    out["Gc"] = left3(np.concatenate([(Se @ Me)[own][:, grid], (Se @ Ne)[own][:, grid]], 1), "c")
    same = lambda p, ends: (p[:, None] == p[None, :]) | sum(
        ((p[:, None] == a) & (p[None, :] == b)) | ((p[:, None] == b) & (p[None, :] == a)) for a, b in ends
    ).astype(bool)
    T = (same(cx, [(-1, 0), (XC - 1, XC)]) & same(cy, [(-1, 0), (YC - 1, YC)])).astype(np.float32).astype(BF16)
    out["T"] = np.concatenate([T, T], 1)
    pick = np.zeros((len(cx), 80))
    for i, (x, y) in enumerate(zip(cx // NC, cy // NC)):
        pick[i, ((x // EX + 1) * 3 + y // EY + 1) * 8 + (x % EX) * EY + y % EY] = 1.0
    out["Pc"] = np.concatenate([pick.astype(np.float32).astype(BF16)] * 3, 1)
    Jxy = blocks(EX, np.kron(J, blocks(EY, J)))
    out["Bj"] = right3(np.concatenate([JZ.T @ Wz @ Sz, JZ.T @ Kz @ Sz, JZ.T], 1), "d")
    sel = np.concatenate([np.arange(EX * ROWS), F])
    JM, JN = (SM @ Jxy)[sel], (SN @ Jxy)[sel]
    out["Gj"] = left3(np.concatenate([JM, JN], 1), "d")
    out["Gp"] = left3(Jxy, "d")
    fine_x, fine_y = np.divmod(np.arange(EX * ROWS), YF)
    places = {"f": (np.concatenate([fine_x, F // YF]), np.concatenate([fine_y, F % YF])), "c": (cx, cy)}
    for name, degree in (("f", ORDER), ("c", COARSE_ORDER)):
        n = degree + 1
        _, w, K = gll_tables(degree)
        kd = np.diag(K)
        S = sum_matrix(EZ, n)
        spread_w = np.zeros((128, EZ * n))
        spread_k = np.zeros((128, EZ * n))
        for ez in range(EZ):
            spread_w[ez, ez * n : (ez + 1) * n] = w
            spread_k[ez, ez * n : (ez + 1) * n] = kd
        out["Bd" + name] = right3(np.concatenate([spread_w @ S, spread_k @ S], 1), "g")
        left = np.zeros((len(places[name][0]), 2, 80))
        for i, (x, y) in enumerate(zip(*places[name])):
            xs = [(x // n, x % n)]
            if x % n == 0:
                xs.append((x // n - 1, n - 1))
            if x % n == n - 1:
                xs.append((x // n + 1, 0))
            ys = [(y // n, y % n)]
            if y % n == 0:
                ys.append((y // n - 1, n - 1))
            if y % n == n - 1:
                ys.append((y // n + 1, 0))
            for ex, a in xs:
                for ey, b in ys:
                    col = ((ex // EX + 1) * 3 + ey // EY + 1) * 8 + (ex % EX) * EY + ey % EY
                    left[i, 0, col] += kd[a] * w[b] + w[a] * kd[b]
                    left[i, 1, col] += w[a] * w[b]
        left = left.reshape(len(left), 160)
        out["Gd" + name] = left3(left, "g")
    spread = np.zeros((128, ZF + ZC))
    for ez in range(EZ):
        spread[ez, ez * N : (ez + 1) * N] = 1.0
        spread[ez, ZF + ez * NC : ZF + (ez + 1) * NC] = 1.0
    out["Bs"] = np.concatenate([spread.astype(np.float32).astype(BF16)] * 3, 0)
    return out


def dot(a, b):
    return jnp.dot(a, b, preferred_element_type=F32)


def split(x, n):
    out = []
    for i in range(1 + max(i for i, _ in TERMS[:n])):
        out.append(x.astype(BF16))
        x = x - out[-1].astype(F32)
    return out


def rmul(x, b, n, cols=slice(None)):
    p = split(x, n)
    x3 = jnp.concatenate([p[i] for i, _ in TERMS[:n]], 1)
    return dot(x3, b[: x3.shape[1], cols])


def lmul(g, *parts, n, rows=slice(None)):
    split_parts = [split(x, n) for x in parts]
    x3 = jnp.concatenate([p[i] for i, _ in TERMS[:n] for p in split_parts], 0)
    return dot(g[rows, : x3.shape[0]], x3)


def kernel_body(shape, names, rhs_ref, coef_ref, *refs):
    gxn, gyn = shape
    n_const = len(names)
    const_hbm = dict(zip(names, refs[:n_const]))
    sol_ref, res_ref = refs[n_const : n_const + 2]
    rest = refs[n_const + 2 :]
    const = dict(zip(names, rest[:n_const]))
    (Fr, Zr, Dr, Cr, DFr, DcFr, Lr, Sr, Rr, Ar, FXr, FFr, PHr, Hr, Wr, WLr, WFr, WLFr,
     Dc_r, Cc_r, cpad, tiles,
     sx, sy, rx, ry, rc, cs, cr, dots, d1, d2,
     const_sem, send_sem, recv_sem, csend_sem, crecv_sem, tsend_sem, trecv_sem, dsend_sem, drecv_sem) = rest[n_const:]

    inv_center, a_f, k_f = cheb_numbers(ORDER)
    inv_center_c, a_c, k_c = cheb_numbers(COARSE_ORDER)
    px, py = lax.axis_index("gx"), lax.axis_index("gy")
    XF, XC, OWN = EX * N, EX * NC, EX * ROWS_C

    def at(dx, dy):
        return (lax.rem(px + dx + gxn, gxn), lax.rem(py + dy + gyn, gyn))

    def inside(dx, dy):
        ok = None
        for p, d, n in ((px, dx, gxn), (py, dy, gyn)):
            if d:
                here = (p > 0) if d < 0 else (p < n - 1)
                ok = here if ok is None else ok & here
        return ok

    corners = [(dx, dy) for dx in (-1, 1) for dy in (-1, 1)]
    around = corners + [(-1, 0), (1, 0), (0, -1), (0, 1)]
    stages = [
        [(px, lax.rem(py + d, gyn)) for d in range(1, gyn)],
        [(lax.rem(px + d, gxn), py) for d in range(1, gxn)],
    ]

    copies = [pltpu.make_async_copy(const_hbm[m], const[m], const_sem.at[i]) for i, m in enumerate(names)]
    for c in copies:
        c.start()

    for ref in (rx, ry, rc, cr, tiles, cpad):
        ref[...] = jnp.zeros_like(ref)
    cpad[0:EY, 0:EZ] = coef_ref[0]
    cpad[EY : 2 * EY, 0:EZ] = coef_ref[1]

    barrier = pltpu.get_barrier_semaphore()
    expected = 0
    for d in around:
        pl.when(inside(*d))(
            lambda d=d: pl.semaphore_signal(barrier, inc=1, device_id=at(*d), device_id_type=MESH)
        )
        expected = expected + inside(*d).astype(jnp.int32)
    for stage in stages:
        for p in stage:
            pl.semaphore_signal(barrier, inc=1, device_id=p, device_id_type=MESH)
        expected = expected + len(stage)

    def local_sum(v):
        rows = lax.broadcasted_iota(jnp.int32, v.shape, 0)
        lanes = lax.broadcasted_iota(jnp.int32, v.shape, 1)
        y = lax.rem(rows, YF)
        up = (lax.rem(y, N) == N - 1) & (y != YF - 1)
        down = (lax.rem(y, N) == 0) & (y != 0)
        v = v + jnp.where(up, pltpu.roll(v, ROWS - 1, 0), 0.0) + jnp.where(down, pltpu.roll(v, 1, 0), 0.0)
        up = (lax.rem(lanes, N) == N - 1) & (lanes != ZF - 1)
        down = (lax.rem(lanes, N) == 0) & (lanes != 0)
        return v + jnp.where(up, pltpu.roll(v, ZF - 1, 1), 0.0) + jnp.where(down, pltpu.roll(v, 1, 1), 0.0)

    def middle(ref, *index):
        total = ref[(*index, 0, pl.ds(ROWS - YF, YF))] + ref[(*index, 1, pl.ds(0, YF))]
        ref[(*index, 0, pl.ds(ROWS - YF, YF))] = total
        ref[(*index, 1, pl.ds(0, YF))] = total

    for e in range(EX):
        Fr[0, e] = local_sum(rhs_ref[e])
    middle(Fr, 0)
    sx[0, 0] = Fr[0, 0, 0:YF]
    sx[0, 1] = Fr[0, 1, ROWS - YF : ROWS]
    for x in range(XF):
        e, r = x // N, (x % N) * YF
        sy[0, 0, x : x + 1] = Fr[0, e, r : r + 1]
        sy[0, 1, x : x + 1] = Fr[0, e, r + YF - 1 : r + YF]

    class Exchange:
        def __init__(self, plan, send, recv):
            self.plan = [
                (pltpu.make_async_remote_copy(
                    src_ref=s, dst_ref=t, send_sem=send(j), recv_sem=recv(j), device_id=at(*d), device_id_type=MESH,
                ), inside(*d), inside(-d[0], -d[1]))
                for j, (s, t, d) in enumerate(plan)
            ]

        def start(self):
            for c, to, _ in self.plan:
                pl.when(to)(c.start)

        def arrive(self):
            for c, _, come in self.plan:
                pl.when(come)(c.wait_recv)

        def drain(self):
            for c, to, _ in self.plan:
                pl.when(to)(c.wait_send)

    def fine(i):
        one = lambda r: pl.ds(r, 1)
        plan = [
            (sy.at[i, 0, one(0)], rc.at[i, 1, one(XF - 1)], (-1, -1)),
            (sy.at[i, 1, one(0)], rc.at[i, 0, one(XF - 1)], (-1, 1)),
            (sy.at[i, 0, one(XF - 1)], rc.at[i, 1, one(0)], (1, -1)),
            (sy.at[i, 1, one(XF - 1)], rc.at[i, 0, one(0)], (1, 1)),
            (sx.at[i, 0], rx.at[i, 1], (-1, 0)),
            (sx.at[i, 1], rx.at[i, 0], (1, 0)),
            (sy.at[i, 0], ry.at[i, 1], (0, -1)),
            (sy.at[i, 1], ry.at[i, 0], (0, 1)),
        ]
        return Exchange(plan, lambda j: send_sem.at[i, j], lambda j: recv_sem.at[i, j])

    def coarse(k):
        h, q = ROWS_C, NC * NC
        y0, y1 = OWN, OWN + XC * NC
        c0 = 2 * h + 4 * q
        src = lambda a, n: cs.at[k, pl.ds(a, n)]
        dst = lambda a, n: cr.at[k, pl.ds(a, n)]
        plan = [
            (src(y0, q), dst(c0 + 3 * q, q), (-1, -1)),
            (src(y1, q), dst(c0 + 2 * q, q), (-1, 1)),
            (src(y0 + q, q), dst(c0 + q, q), (1, -1)),
            (src(y1 + q, q), dst(c0, q), (1, 1)),
            (src(0, h), dst(h, h), (-1, 0)),
            (src(h, h), dst(0, h), (1, 0)),
            (src(y0, 2 * q), dst(2 * h + 2 * q, 2 * q), (0, -1)),
            (src(y1, 2 * q), dst(2 * h, 2 * q), (0, 1)),
        ]
        return Exchange(plan, lambda j: csend_sem.at[k, j], lambda j: crecv_sem.at[k, j])

    pl.semaphore_wait(barrier, expected)

    tile_plan = []
    for dx, dy in around:
        slot = ((1 - dx) * 3 + (1 - dy)) * 8
        tile_plan.append((cpad, tiles.at[pl.ds(slot, 8)], (dx, dy)))
    tile_exchange = Exchange(tile_plan, lambda j: tsend_sem.at[j], lambda j: trecv_sem.at[j])
    tile_exchange.start()
    fine(0).start()
    tiles[32:40] = cpad[...]

    for c in copies:
        c.wait()

    def spread(x):
        h1 = x.astype(BF16)
        r1 = x - h1.astype(F32)
        h2 = r1.astype(BF16)
        return [h1, h2, (r1 - h2.astype(F32)).astype(BF16)]

    spread_own = dot(jnp.concatenate(spread(cpad[...]), 1), const["Bs"][...])
    for e in range(EX):
        lines = [spread_own[e * EY + ey : e * EY + ey + 1] for ey in range(EY)]
        cf = [jnp.broadcast_to(l[:, :ZF], (N, ZF)) for l in lines]
        one = jnp.concatenate(cf, 0)
        Cr[e] = jnp.concatenate([one] * N, 0)
        FXr[0, e * YF : (e + 1) * YF] = one
        FXr[0, 2 * YF + e * N : 2 * YF + (e + 1) * N] = cf[0]
        FXr[0, 2 * YF + (EX + e) * N : 2 * YF + (EX + e + 1) * N] = cf[EY - 1]

    rows = lax.broadcasted_iota(jnp.int32, (ROWS, ZF), 0)
    lanes = lax.broadcasted_iota(jnp.int32, (ROWS, ZF), 1)
    xr, yr = rows // YF, lax.rem(rows, YF)
    frow = lax.broadcasted_iota(jnp.int32, (96, ZF), 0)
    flane = lax.broadcasted_iota(jnp.int32, (96, ZF), 1)
    fx = jnp.where(frow < YF, 0, jnp.where(frow < 2 * YF, XF - 1, lax.rem(frow, XF)))
    fy = jnp.where(frow < 2 * YF, lax.rem(frow, YF), jnp.where(frow < 2 * YF + XF, 0, YF - 1))

    def edge(i, count=0):
        e = (lax.rem(i, N) == 0) | (lax.rem(i, N) == N - 1)
        return jnp.where(e & (i != 0) & (i != count - 1) if count else e, 0.5, 1.0)

    Wr[...] = edge(lanes) * edge(yr) * edge(xr)
    WLr[...] = edge(lanes) * edge(yr, YF)
    WFr[...] = edge(flane) * edge(fx) * edge(fy)
    WLFr[...] = edge(flane) * edge(fx, XF) * edge(fy, YF)

    tile_exchange.arrive()
    ext = tiles[...]
    pd = rmul(ext, const["Bdf"], HOW["g"])
    diag = lmul(const["Gdf"], pd[:, :ZF], pd[:, ZF:], n=HOW["g"])

    def mask_of(x, y, z, n):
        inner = (x > 0) & (x < gxn * EX * n - 1) & (y > 0) & (y < gyn * EY * n - 1)
        return inner & (z != 0) & (z != EZ * n - 1)

    for e in range(EX):
        keep = mask_of(px * XF + e * N + xr, py * YF + yr, lanes, N)
        Dr[e] = jnp.where(keep, 1.0 / diag[e * ROWS : (e + 1) * ROWS], 0.0)
    keep = mask_of(px * XF + fx, py * YF + fy, flane, N)
    df = jnp.where(keep, 1.0 / diag[EX * ROWS :], 0.0)
    DFr[...] = df
    DcFr[...] = df * FXr[0]
    pdc = rmul(ext, const["Bdc"], HOW["g"])
    diag_c = lmul(const["Gdc"], pdc[:, :ZC], pdc[:, ZC:], n=HOW["g"])
    crow = lax.broadcasted_iota(jnp.int32, (384, ZC), 0)
    clane = lax.broadcasted_iota(jnp.int32, (384, ZC), 1)

    def place(r, width, x0, y0):
        return (x0 + r // width, y0 + lax.rem(r, width))

    cx, cy = place(crow, YC, 0, 0)
    base = OWN
    for count, width, x0, y0 in (
        (ROWS_C, YC, -NC, 0), (ROWS_C, YC, XC, 0), (XC * NC, NC, 0, -NC), (XC * NC, NC, 0, YC),
        (16, NC, -NC, -NC), (16, NC, -NC, YC), (16, NC, XC, -NC), (16, NC, XC, YC),
    ):
        nx, ny = place(crow - base, width, x0, y0)
        cx, cy = jnp.where(crow >= base, nx, cx), jnp.where(crow >= base, ny, cy)
        base += count
    keep = mask_of(px * XC + cx, py * YC + cy, clane, NC)
    Dc_r[...] = jnp.where(keep, 1.0 / diag_c, 0.0)
    lines = dot(jnp.concatenate(spread(ext), 1), const["Bs"][:, ZF:])
    Cc_r[...] = dot(const["Pc"][...], jnp.concatenate(spread(lines), 0))

    def halo(i):
        fine(i).arrive()
        return jnp.concatenate([rx[i, 0], rx[i, 1], ry[i, 0] + rc[i, 0], ry[i, 1] + rc[i, 1]], 0)

    def add_faces(ref, index, h):
        ref[(*index, 0, pl.ds(0, YF))] += h[0:YF]
        ref[(*index, 1, pl.ds(ROWS - YF, YF))] += h[YF : 2 * YF]
        for x in range(XF):
            e, r = x // N, (x % N) * YF
            ref[(*index, e, pl.ds(r, 1))] += h[2 * YF + x : 2 * YF + x + 1]
            b = 2 * YF + XF + x
            ref[(*index, e, pl.ds(r + YF - 1, 1))] += h[b : b + 1]

    def bulk(values, n):
        y0 = None
        for e in range(EX):
            p = rmul(values(e), const["Bf"], n)
            o = lmul(const[f"Gb{e}"], p[:, :ZF], p[:, ZF:], n=n)
            Lr[e] = o[:ROWS]
            FXr[1, e * YF : (e + 1) * YF] = o[ROWS : ROWS + YF]
            y0 = o[ROWS + YF :] if e == 0 else y0 + o[ROWS + YF :]
        FXr[1, 2 * YF :] = y0

    def face_z(hs, n):
        return rmul(hs, const["Bf"], n)

    def send_faces(i, faces):
        sx[i, 0] = faces[0:YF]
        sx[i, 1] = faces[YF : 2 * YF]
        sy[i, 0] = faces[2 * YF : 2 * YF + XF]
        sy[i, 1] = faces[2 * YF + XF :]
        fine(i).start()

    def face_to_face(ph, n):
        return lmul(const["F2F"], ph[:, :ZF], ph[:, ZF:], n=n)

    def face_to_all(ph, n):
        for e in range(EX):
            part = jnp.concatenate([ph[e * YF : (e + 1) * YF], ph[2 * YF :]], 0)
            Lr[e] += lmul(const[f"F2A{e}"], part[:, :ZF], part[:, ZF:], n=n)
        middle(Lr)

    def finish(k):
        add_faces(Zr, (k,), (-k_f) * DFr[...] * Hr[...])
        face_to_all(PHr[...], HOW["h"])
        for e in range(EX):
            Fr[k + 1, e] = Lr[e]

    def total(x):
        x = jnp.sum(x, axis=0, keepdims=True)
        return x[:, : ZF // 2] + x[:, ZF // 2 :]

    def cycle(k, carry):
        pl.when(k > 0)(lambda: finish(k - 1))
        bulk(lambda e: Cr[e] * (Dr[e] * inv_center) * Fr[k, e], HOW["a"])
        h = halo(4 * k)
        ph = face_z(DcFr[...] * inv_center * h, HOW["a"])
        send_faces(4 * k + 1, FXr[1] + face_to_face(ph, HOW["a"]))
        add_faces(Fr, (k,), h)
        FFr[k, 0:YF] = Fr[k, 0, 0:YF]
        FFr[k, YF : 2 * YF] = Fr[k, 1, ROWS - YF : ROWS]
        for x in range(XF):
            e, r = x // N, (x % N) * YF
            FFr[k, 2 * YF + x : 2 * YF + x + 1] = Fr[k, e, r : r + 1]
            b = 2 * YF + XF + x
            FFr[k, b : b + 1] = Fr[k, e, r + YF - 1 : r + YF]
        face_to_all(ph, HOW["a"])
        gl = None
        for e in range(EX):
            s = Dr[e] * (a_f * Fr[k, e] - k_f * Lr[e])
            Sr[e] = s
            p = rmul(Cr[e] * s, const["Br"], HOW["b"])
            Ar[e, :, 0:ZC] = rmul(Fr[k, e], const["Bw"], HOW["b"])
            o = lmul(const[f"Gr{e}"], p[:, :ZC], p[:, ZC:], n=HOW["b"])
            gl = o if e == 0 else gl + o
        gl = lmul(const["Gw"], Ar[0, :, 0:ZC], Ar[1, :, 0:ZC], n=HOW["b"]) - gl
        h = halo(4 * k + 1)
        hs = (-k_f) * DcFr[...] * h
        pr = rmul(hs, const["Br"], HOW["b"])
        gl = gl - lmul(const["F2R"], pr[:, :ZC], pr[:, ZC:], n=HOW["b"])
        cs[k] = gl
        coarse(k).start()
        bulk(lambda e: Cr[e] * Sr[e], HOW["s"])
        ph = face_z(hs, HOW["s"])
        face_to_all(ph, HOW["s"])
        FXr[1] = FXr[1] + face_to_face(ph, HOW["s"])
        add_faces(Sr, (), (-k_f) * DFr[...] * h)
        coarse(k).arrive()
        g1, g2 = split(jnp.concatenate([cs[k, 0:OWN], cr[k]], 0), 3)
        g = dot(const["T"][...], jnp.concatenate([g1, g2], 0))
        p = rmul(Cc_r[...] * (Dc_r[...] * inv_center_c) * g, const["Bc"], HOW["c"])
        o = lmul(const["Gc"], p[:, :ZC], p[:, ZC:], n=HOW["c"])
        fix = Dc_r[0:OWN] * (a_c * g[0:OWN] - k_c * o)
        p = rmul(Cc_r[0:OWN] * fix, const["Bj"], HOW["d"], slice(0, 2 * ZF))
        o = lmul(const["Gj"], p[:, :ZF], p[:, ZF:], n=HOW["d"], rows=slice(EX * ROWS, EX * ROWS + 96))
        send_faces(4 * k + 2, FXr[1] + o)
        o = lmul(const["Gj"], p[:, :ZF], p[:, ZF:], n=HOW["d"], rows=slice(0, EX * ROWS))
        p = rmul(fix, const["Bj"], HOW["d"], slice(2 * ZF, 3 * ZF))
        up = lmul(const["Gp"], p, n=HOW["d"])
        for e in range(EX):
            part = slice(e * ROWS, (e + 1) * ROWS)
            Sr[e] = Sr[e] + up[part]
            Rr[e] = Fr[k, e] - Lr[e] - o[part]
        bulk(lambda e: Cr[e] * (Dr[e] * inv_center) * Rr[e], HOW["e"])
        h = halo(4 * k + 2)
        ph = face_z((-inv_center) * DcFr[...] * h, HOW["e"])
        send_faces(4 * k + 3, FXr[1] + face_to_face(ph, HOW["e"]))
        add_faces(Rr, (), -h)
        face_to_all(ph, HOW["e"])
        for e in range(EX):
            Zr[k, e] = Sr[e] + Dr[e] * (a_f * Rr[e] - k_f * Lr[e])
        bulk(lambda e: Cr[e] * Zr[k, e], HOW["f"])
        sums = [0.0] * 3
        for e in range(EX):
            z = Zr[k, e]
            wz = Wr[...] * z
            for i, t in enumerate((Fr[0, e] * wz, Fr[k, e] * wz, WLr[...] * Lr[e] * z)):
                sums[i] = sums[i] + total(t)
        h = halo(4 * k + 3)
        delta = (-k_f) * DFr[...] * h
        ph = face_z((-k_f) * DcFr[...] * h, HOW["h"])
        ff = face_to_face(ph, HOW["h"])
        send_faces(4 * k + 4, FXr[1] + ff)
        wd = WFr[...] * delta
        faces = (FFr[0] * wd, FFr[k] * wd, WLFr[...] * delta * (2.0 * FXr[1] + ff))
        for i, t in enumerate(faces):
            dots[k, i : i + 1] = sums[i] + total(t)
        PHr[...] = ph
        Hr[...] = h
        return carry

    lax.fori_loop(0, 2, cycle, 0)

    def reduce_stage(buf, stage, base):
        return [
            pltpu.make_async_remote_copy(
                src_ref=buf.at[0], dst_ref=buf.at[j + 1], send_sem=dsend_sem.at[base + j], recv_sem=drecv_sem.at[base + j],
                device_id=p, device_id_type=MESH,
            )
            for j, p in enumerate(stage)
        ]

    def summed(buf, stage, n):
        for c in stage:
            c.wait_recv()
        out = buf[0]
        for j in range(n):
            out = out + buf[j + 1]
        return out

    d1[0, 0:3] = dots[0, 0:3]
    d1[0, 3:6] = dots[1, 0:3]
    d1[0, 6:8] = jnp.zeros((2, 128), F32)
    stage1 = reduce_stage(d1, stages[0], 0)
    stage2 = reduce_stage(d2, stages[1], len(stage1))
    for c in stage1:
        c.start()
    finish(1)
    d2[0] = summed(d1, stage1, len(stage1))
    for c in stage2:
        c.start()
    h = halo(8)
    add_faces(Fr, (2,), h)
    lanes_sum = jnp.sum(summed(d2, stage2, len(stage2)), axis=1, keepdims=True)
    pick = lambda i: lanes_sum[i : i + 1, 0:1]
    rz0, c00 = pick(1), pick(2)
    r0u, wu, uv = pick(3), pick(4), pick(5)
    alpha0 = rz0 / c00
    rz1 = alpha0 * (alpha0 * wu - r0u)
    beta1 = 1.0 + rz1 / rz0
    curve = beta1 * beta1 * c00 - 2.0 * beta1 * alpha0 * wu + alpha0 * alpha0 * uv
    alpha1 = rz1 / curve
    c_z = alpha0 + alpha1 * beta1
    c_u = alpha1 * alpha0
    for e in range(EX):
        sol_ref[e] = c_z * Zr[0, e] - c_u * Zr[1, e]
        res_ref[e] = jnp.where(Dr[e] > 0.0, Fr[0, e] - c_z * Fr[1, e] + c_u * Fr[2, e], 0.0)

    tile_exchange.drain()
    for c in stage1 + stage2:
        c.wait_send()

    def drain(i, carry):
        fine(i).drain()
        return carry

    lax.fori_loop(0, 9, drain, 0)
    for k in range(2):
        coarse(k).drain()


def solution(mesh):
    gxn, gyn = mesh.shape["gx"], mesh.shape["gy"]
    table = constants()
    names = tuple(table)
    n_dots = gyn - 1 + gxn - 1

    def per_device(right_side, coefficient):
        rhs = right_side.reshape(EX, ROWS, ZF)
        field = (EX, ROWS, ZF)
        vm = lambda *s: pltpu.VMEM(s, F32)
        dma = lambda *s: pltpu.SemaphoreType.DMA(s)
        face = (96, ZF)
        scratch = [pltpu.VMEM(table[m].shape, BF16) for m in names]
        scratch += [
            vm(3, *field), vm(2, *field), vm(*field), vm(*field), vm(*face), vm(*face),
            vm(*field), vm(*field), vm(*field), vm(*field), vm(2, *face), vm(2, *face), vm(96, 2 * ZF), vm(*face),
            vm(ROWS, ZF), vm(ROWS, ZF), vm(*face), vm(*face),
            vm(384, ZC), vm(384, ZC), vm(8, 128), vm(80, 128),
            vm(9, 2, YF, ZF), vm(9, 2, EX * N, ZF), vm(9, 2, YF, ZF), vm(9, 2, EX * N, ZF), vm(9, 2, EX * N, ZF),
            vm(2, 192, ZC), vm(2, 256, ZC),
            vm(2, 8, 128), vm(gyn, 8, 128), vm(gxn, 8, 128),
            dma(len(names)), dma(9, 8), dma(9, 8), dma(2, 8), dma(2, 8), dma(8), dma(8), dma(n_dots), dma(n_dots),
        ]
        sol, res = pl.pallas_call(
            functools.partial(kernel_body, (gxn, gyn), names),
            out_shape=[jax.ShapeDtypeStruct(field, F32)] * 2,
            in_specs=[pl.BlockSpec(memory_space=pltpu.VMEM)] * 2 + [pl.BlockSpec(memory_space=pl.ANY)] * len(names),
            out_specs=[pl.BlockSpec(memory_space=pltpu.VMEM)] * 2,
            scratch_shapes=scratch,
            compiler_params=pltpu.CompilerParams(
                collective_id=0, has_side_effects=True, vmem_limit_bytes=56 * 2**20
            ),
        )(rhs, coefficient, *[jnp.asarray(table[m]) for m in names])
        return sol.reshape(right_side.shape), res.reshape(right_side.shape)

    spec = P("gx", "gy", None)
    return jax.shard_map(
        per_device, mesh=mesh, in_specs=(spec, spec), out_specs=(spec, spec), check_vma=False
    )
```

time: 100 us -> 80.3 us (0.80)
  Pallas kernels: 95.7 us -> 75.8 us
    pallas_call x1, Pallas kernels: 95.7 us -> 75.8 us  [per_device(): pl.pallas_call(functools.partial(kernel_body, (gxn, gyn), names), out_sha...]
where the time goes in v2:
time: 80.3 us; the launch traced here: 80.2 us
  Pallas kernels  75.8 us (94%)
  local copies, waits for them, and re-layouts  3.76 us (5%)
    pallas_call x1, Pallas kernels, per_device(): pl.pallas_call(functools.partial(kernel_body, (gxn, gyn), names), out_sha...  75.8 us
    unnamed x2, local copies, waits for them, and re-layouts  3.76 us

profile of v2, /device:TPU:1, one launch (start us, length us, event | category | flops | bytes accessed | tf_op | source)
XLA Modules:
  0.0 80.2 jit_solution(15199009268254521991)
XLA Ops:
  0.6 75.8 %shard_map.257 = (f32[2,256,256]{2,1,0:T(8,128)}, f32[2,256,256]{2,1,0:T(8,128)}) custom-call(f32[2,256,256]{2,1,0:T(8,128)} %bitcast.3, f32[2,4,32]{2,1,0:T(4,128)} %coef_ref.1, bf16[1536,512]{1,0:T(8,128)(2,1)} %constant.48.clone.refs_0_, bf16[320,3072]{1,0:T(8,128)(2,1)} %constant.49.clone.refs_1_, bf16[320,3072]{1,0:T(8,128)(2,1)} %constant.50.clone.refs_2_, ...), custom_call_target="tpu_custom_call" | custom-call | tf_op jit(solution)/shard_map/pallas_call | solution.py:722
  76.4 1.9 %copy.30 = f32[16,32,256]{2,1,0:T(8,128)} copy(f32[16,32,256]{2,1,0:T(8,128)} %bitcast.5) | data formatting | bytes 1048576
  78.3 1.9 %copy.31 = f32[16,32,256]{2,1,0:T(8,128)} copy(f32[16,32,256]{2,1,0:T(8,128)} %bitcast.4) | data formatting | bytes 1048576

commit v3 on v2

--- a/solution.py
+++ b/solution.py
@@ -151,6 +151,18 @@
     return np.array([p[0] for p in both]), np.array([p[1] for p in both])
 
 
+def coarse_pairs():
+    x, y = coarse_places()
+    row = {p: i for i, p in enumerate(zip(x.tolist(), y.tolist()))}
+    XC, out = EX * NC, []
+    for a, b in ((-1, 0), (XC - 1, XC)):
+        for first, n in ((-NC, NC), (0, YC), (YC, NC)):
+            out.append((row[a, first], row[b, first], n))
+    for a, b in ((-1, 0), (YC - 1, YC)):
+        out += [(row[i, a], row[i, b], 1) for i in range(-NC, XC + NC)]
+    return out
+
+
 @functools.cache
 def constants():
     J = interpolation_matrix(ORDER, COARSE_ORDER)
@@ -163,14 +175,18 @@
     SM, SN = Sxy @ Mf, Sxy @ Nf
     F = face_rows(N)
     out["Bf"] = right3(np.concatenate([Wz @ Sz, Kz @ Sz], 1))
+    _, w, K = gll_tables(ORDER)
+    wxy, wz = np.kron(w, np.tile(w, EY)), np.tile(w, EZ)
+    out["Mh"] = left3(M0 / wxy[:, None])
+    out["Kh"] = right3(Kz / wz[None, :])
+    out["w3"] = (wxy[:, None] * wz[None, :]).astype(np.float32)
+    y, z = np.arange(ROWS) % YF, np.arange(ZF)
+    wide = lambda m, shape: np.broadcast_to(m, shape).astype(np.float32)
+    out["yu"] = wide(((y % N == N - 1) & (y != YF - 1))[:, None], (ROWS, 128))
+    out["yd"] = wide(((y % N == 0) & (y != 0))[:, None], (ROWS, 128))
+    out["zu"] = wide(((z % N == N - 1) & (z != ZF - 1))[None, :], (8, ZF))
+    out["zd"] = wide(((z % N == 0) & (z != 0))[None, :], (8, ZF))
     Sy = np.kron(np.eye(EX * N), sum_matrix(EY, N))
-    for e in range(EX):
-        cols = slice(e * ROWS, (e + 1) * ROWS)
-        full = np.concatenate([(Sy @ Mf)[cols, cols], (Sy @ Nf)[cols, cols]], 1)
-        xf = F[e * YF : (e + 1) * YF]
-        face = np.concatenate([xf, F[2 * YF :]])
-        packed = np.concatenate([SM[face][:, cols], SN[face][:, cols]], 1)
-        out[f"Gb{e}"] = left3(np.concatenate([full, packed], 0))
     out["F2F"] = left3(np.concatenate([SM[F][:, F], SN[F][:, F]], 1))
     for e in range(EX):
         rows = slice(e * ROWS, (e + 1) * ROWS)
@@ -197,7 +213,7 @@
     out["Gw"] = left3(RW, "b")
     _, wc, Kc = gll_tables(COARSE_ORDER)
     Wzc, Kzc = np.diag(np.tile(wc, EZ)), blocks(EZ, Kc)
-    out["Bc"] = right3(np.concatenate([Wzc @ Szc, Kzc @ Szc], 1), "c")
+    out["Bc"] = right3(np.concatenate([Wzc @ Szc, Kzc @ Szc], 0), "c")
     cx, cy = coarse_places()
     grid = (cx + NC) * (YC + 2 * NC) + cy + NC
     wx4, wy6 = np.diag(np.tile(wc, EX + 2)), np.diag(np.tile(wc, EY + 2))
@@ -205,12 +221,7 @@
     Ne = np.kron(wx4, wy6)
     Se = np.kron(sum_matrix(EX + 2, NC), sum_matrix(EY + 2, NC))
     own = grid[: XC * YC]
-    out["Gc"] = left3(np.concatenate([(Se @ Me)[own][:, grid], (Se @ Ne)[own][:, grid]], 1), "c")
-    same = lambda p, ends: (p[:, None] == p[None, :]) | sum(
-        ((p[:, None] == a) & (p[None, :] == b)) | ((p[:, None] == b) & (p[None, :] == a)) for a, b in ends
-    ).astype(bool)
-    T = (same(cx, [(-1, 0), (XC - 1, XC)]) & same(cy, [(-1, 0), (YC - 1, YC)])).astype(np.float32).astype(BF16)
-    out["T"] = np.concatenate([T, T], 1)
+    out["Gc"] = left3(np.concatenate([(Se @ Me)[own][:, grid], (Se @ Ne)[own][:, grid]], 0), "c")
     pick = np.zeros((len(cx), 80))
     for i, (x, y) in enumerate(zip(cx // NC, cy // NC)):
         pick[i, ((x // EX + 1) * 3 + y // EY + 1) * 8 + (x % EX) * EY + y % EY] = 1.0
@@ -292,7 +303,7 @@
     sol_ref, res_ref = refs[n_const : n_const + 2]
     rest = refs[n_const + 2 :]
     const = dict(zip(names, rest[:n_const]))
-    (Fr, Zr, Dr, Cr, DFr, DcFr, Lr, Sr, Rr, Ar, FXr, FFr, PHr, Hr, Wr, WLr, WFr, WLFr,
+    (Fr, Zr, Dr, Cr, W3r, gr, DFr, DcFr, Lr, Sr, Rr, Ar, FXr, FFr, PHr, Hr, Wr, WLr, WFr, WLFr,
      Dc_r, Cc_r, cpad, tiles,
      sx, sy, rx, ry, rc, cs, cr, dots, d1, d2,
      const_sem, send_sem, recv_sem, csend_sem, crecv_sem, tsend_sem, trecv_sem, dsend_sem, drecv_sem) = rest[n_const:]
@@ -446,6 +457,7 @@
         cf = [jnp.broadcast_to(l[:, :ZF], (N, ZF)) for l in lines]
         one = jnp.concatenate(cf, 0)
         Cr[e] = jnp.concatenate([one] * N, 0)
+        W3r[e] = Cr[e] * const["w3"][...]
         FXr[0, e * YF : (e + 1) * YF] = one
         FXr[0, 2 * YF + e * N : 2 * YF + (e + 1) * N] = cf[0]
         FXr[0, 2 * YF + (EX + e) * N : 2 * YF + (EX + e + 1) * N] = cf[EY - 1]
@@ -518,15 +530,27 @@
             b = 2 * YF + XF + x
             ref[(*index, e, pl.ds(r + YF - 1, 1))] += h[b : b + 1]
 
+    def sums_inside(v):
+        wide = lambda name: jnp.concatenate([const[name][...]] * 2, 1)
+        v = v + wide("yu") * pltpu.roll(v, ROWS - 1, 0) + wide("yd") * pltpu.roll(v, 1, 0)
+        return v + const["zu"][0:1] * pltpu.roll(v, ZF - 1, 1) + const["zd"][0:1] * pltpu.roll(v, 1, 1)
+
     def bulk(values, n):
-        y0 = None
         for e in range(EX):
-            p = rmul(values(e), const["Bf"], n)
-            o = lmul(const[f"Gb{e}"], p[:, :ZF], p[:, ZF:], n=n)
-            Lr[e] = o[:ROWS]
-            FXr[1, e * YF : (e + 1) * YF] = o[ROWS : ROWS + YF]
-            y0 = o[ROWS + YF :] if e == 0 else y0 + o[ROWS + YF :]
-        FXr[1, 2 * YF :] = y0
+            p = split(values(e), n)
+            p = [p[i] for i, _ in TERMS[:n]]
+            t = dot(const["Mh"][:, : n * ROWS], jnp.concatenate(p, 0))
+            t = t + dot(jnp.concatenate(p, 1), const["Kh"][: n * ZF])
+            Lr[e] = sums_inside(W3r[e] * t)
+        FXr[1, 0:YF] = Lr[0, 0:YF]
+        FXr[1, YF : 2 * YF] = Lr[1, ROWS - YF : ROWS]
+        for side, y in ((2 * YF, 0), (2 * YF + XF, YF - 1)):
+            for x in range(XF):
+                e, r = x // N, (x % N) * YF + y
+                FXr[1, side + x : side + x + 1] = Lr[e, r : r + 1]
+            both = Lr[0, ROWS - YF + y : ROWS - YF + y + 1] + Lr[1, y : y + 1]
+            FXr[1, side + N - 1 : side + N] = both
+            FXr[1, side + N : side + N + 1] = both
 
     def face_z(hs, n):
         return rmul(hs, const["Bf"], n)
@@ -559,7 +583,7 @@
 
     def cycle(k, carry):
         pl.when(k > 0)(lambda: finish(k - 1))
-        bulk(lambda e: Cr[e] * (Dr[e] * inv_center) * Fr[k, e], HOW["a"])
+        bulk(lambda e: (Dr[e] * inv_center) * Fr[k, e], HOW["a"])
         h = halo(4 * k)
         ph = face_z(DcFr[...] * inv_center * h, HOW["a"])
         send_faces(4 * k + 1, FXr[1] + face_to_face(ph, HOW["a"]))
@@ -587,17 +611,22 @@
         gl = gl - lmul(const["F2R"], pr[:, :ZC], pr[:, ZC:], n=HOW["b"])
         cs[k] = gl
         coarse(k).start()
-        bulk(lambda e: Cr[e] * Sr[e], HOW["s"])
+        gr[0:OWN] = gl[0:OWN]
+        bulk(lambda e: Sr[e], HOW["s"])
         ph = face_z(hs, HOW["s"])
         face_to_all(ph, HOW["s"])
         FXr[1] = FXr[1] + face_to_face(ph, HOW["s"])
         add_faces(Sr, (), (-k_f) * DFr[...] * h)
         coarse(k).arrive()
-        g1, g2 = split(jnp.concatenate([cs[k, 0:OWN], cr[k]], 0), 3)
-        g = dot(const["T"][...], jnp.concatenate([g1, g2], 0))
-        p = rmul(Cc_r[...] * (Dc_r[...] * inv_center_c) * g, const["Bc"], HOW["c"])
-        o = lmul(const["Gc"], p[:, :ZC], p[:, ZC:], n=HOW["c"])
-        fix = Dc_r[0:OWN] * (a_c * g[0:OWN] - k_c * o)
+        gr[OWN:] = cr[k]
+        for a, b, n in coarse_pairs():
+            t = gr[a : a + n] + gr[b : b + n]
+            gr[a : a + n] = t
+            gr[b : b + n] = t
+        p = lmul(const["Gc"], Cc_r[...] * (Dc_r[...] * inv_center_c) * gr[...], n=HOW["c"])
+        o = rmul(jnp.concatenate([p[:OWN], p[OWN:]], 1), const["Bc"], HOW["c"])
+        g = gr[0:OWN]
+        fix = Dc_r[0:OWN] * (a_c * g - k_c * o)
         p = rmul(Cc_r[0:OWN] * fix, const["Bj"], HOW["d"], slice(0, 2 * ZF))
         o = lmul(const["Gj"], p[:, :ZF], p[:, ZF:], n=HOW["d"], rows=slice(EX * ROWS, EX * ROWS + 96))
         send_faces(4 * k + 2, FXr[1] + o)
@@ -608,7 +637,7 @@
             part = slice(e * ROWS, (e + 1) * ROWS)
             Sr[e] = Sr[e] + up[part]
             Rr[e] = Fr[k, e] - Lr[e] - o[part]
-        bulk(lambda e: Cr[e] * (Dr[e] * inv_center) * Rr[e], HOW["e"])
+        bulk(lambda e: (Dr[e] * inv_center) * Rr[e], HOW["e"])
         h = halo(4 * k + 2)
         ph = face_z((-inv_center) * DcFr[...] * h, HOW["e"])
         send_faces(4 * k + 3, FXr[1] + face_to_face(ph, HOW["e"]))
@@ -616,7 +645,7 @@
         face_to_all(ph, HOW["e"])
         for e in range(EX):
             Zr[k, e] = Sr[e] + Dr[e] * (a_f * Rr[e] - k_f * Lr[e])
-        bulk(lambda e: Cr[e] * Zr[k, e], HOW["f"])
+        bulk(lambda e: Zr[k, e], HOW["f"])
         sums = [0.0] * 3
         for e in range(EX):
             z = Zr[k, e]
@@ -708,9 +737,9 @@
         vm = lambda *s: pltpu.VMEM(s, F32)
         dma = lambda *s: pltpu.SemaphoreType.DMA(s)
         face = (96, ZF)
-        scratch = [pltpu.VMEM(table[m].shape, BF16) for m in names]
+        scratch = [pltpu.VMEM(table[m].shape, table[m].dtype) for m in names]
         scratch += [
-            vm(3, *field), vm(2, *field), vm(*field), vm(*field), vm(*face), vm(*face),
+            vm(3, *field), vm(2, *field), vm(*field), vm(*field), vm(*field), vm(384, ZC), vm(*face), vm(*face),
             vm(*field), vm(*field), vm(*field), vm(*field), vm(2, *face), vm(2, *face), vm(96, 2 * ZF), vm(*face),
             vm(ROWS, ZF), vm(ROWS, ZF), vm(*face), vm(*face),
             vm(384, ZC), vm(384, ZC), vm(8, 128), vm(80, 128),
@@ -721,7 +750,7 @@
         ]
         sol, res = pl.pallas_call(
             functools.partial(kernel_body, (gxn, gyn), names),
-            out_shape=[jax.ShapeDtypeStruct(field, F32)] * 2,
+            out_shape=[pltpu.VMEM(field, F32)] * 2,
             in_specs=[pl.BlockSpec(memory_space=pltpu.VMEM)] * 2 + [pl.BlockSpec(memory_space=pl.ANY)] * len(names),
             out_specs=[pl.BlockSpec(memory_space=pltpu.VMEM)] * 2,
             scratch_shapes=scratch,

time: 80.3 us -> 75.4 us (0.939)
  Pallas kernels: 75.8 us -> 73 us
  local copies, waits for them, and re-layouts: 3.76 us -> 1.59 us
    pallas_call x1, Pallas kernels: 75.8 us -> 73 us  [per_device(): pl.pallas_call(functools.partial(kernel_body, (gxn, gyn), names), out_sha...]
    unnamed x2, local copies, waits for them, and re-layouts: 3.76 us -> 1.59 us
where the time goes in v3:
time: 75.4 us; the launch traced here: 75.3 us
  Pallas kernels  73 us (97%)
  local copies, waits for them, and re-layouts  1.59 us (2%)
    pallas_call x1, Pallas kernels, per_device(): pl.pallas_call(functools.partial(kernel_body, (gxn, gyn), names), out_sha...  73 us
    unnamed x2, local copies, waits for them, and re-layouts  1.59 us

profile of v3, /device:TPU:1, one launch (start us, length us, event | category | flops | bytes accessed | tf_op | source)
XLA Modules:
  0.0 75.3 jit_solution(700339817412043109)
XLA Ops:
  0.6 73.0 %shard_map.293 = (f32[2,256,256]{2,1,0:T(8,128)S(1)}, f32[2,256,256]{2,1,0:T(8,128)S(1)}) custom-call(f32[2,256,256]{2,1,0:T(8,128)} %bitcast.5, f32[2,4,32]{2,1,0:T(4,128)} %coef_ref.1, bf16[1536,512]{1,0:T(8,128)(2,1)} %constant.56.clone.refs_0_, bf16[256,1536]{1,0:T(8,128)(2,1)} %constant.57.clone.refs_1_, bf16[1536,256]{1,0:T(8,128)(2,1)} %constant.58.clone.refs_2_, ...), custom_call_target="tpu_custom_call" | custom-call | tf_op jit(solution)/shard_map/pallas_call | solution.py:751
  73.7 0.8 %copy.34 = f32[16,32,256]{2,1,0:T(8,128)} copy(f32[16,32,256]{2,1,0:T(8,128)S(1)} %bitcast.4) | data formatting | bytes 1048576
  74.5 0.8 %copy.35 = f32[16,32,256]{2,1,0:T(8,128)} copy(f32[16,32,256]{2,1,0:T(8,128)S(1)} %bitcast.3) | data formatting | bytes 1048576

commit v4 on v3

--- a/solution.py
+++ b/solution.py
@@ -263,6 +263,10 @@
                     left[i, 0, col] += kd[a] * w[b] + w[a] * kd[b]
                     left[i, 1, col] += w[a] * w[b]
         left = left.reshape(len(left), 160)
+        if name == "f":
+            here = left.reshape(len(left), 2, 80)[: EX * ROWS, :, 32:40].reshape(EX * ROWS, 16)
+            out["Gdo"] = left3(here, "g")
+            left = left[EX * ROWS :]
         out["Gd" + name] = left3(left, "g")
     spread = np.zeros((128, ZF + ZC))
     for ez in range(EZ):
@@ -304,7 +308,7 @@
     rest = refs[n_const + 2 :]
     const = dict(zip(names, rest[:n_const]))
     (Fr, Zr, Dr, Cr, W3r, gr, DFr, DcFr, Lr, Sr, Rr, Ar, FXr, FFr, PHr, Hr, Wr, WLr, WFr, WLFr,
-     Dc_r, Cc_r, cpad, tiles,
+     Dc_r, Cc_r, cpad, coef, tiles,
      sx, sy, rx, ry, rc, cs, cr, dots, d1, d2,
      const_sem, send_sem, recv_sem, csend_sem, crecv_sem, tsend_sem, trecv_sem, dsend_sem, drecv_sem) = rest[n_const:]
 
@@ -332,13 +336,15 @@
     ]
 
     copies = [pltpu.make_async_copy(const_hbm[m], const[m], const_sem.at[i]) for i, m in enumerate(names)]
+    load_rhs = pltpu.make_async_copy(rhs_ref, Ar, const_sem.at[n_const])
+    load_coef = pltpu.make_async_copy(coef_ref, coef, const_sem.at[n_const + 1])
+    load_rhs.start()
+    load_coef.start()
     for c in copies:
         c.start()
 
     for ref in (rx, ry, rc, cr, tiles, cpad):
         ref[...] = jnp.zeros_like(ref)
-    cpad[0:EY, 0:EZ] = coef_ref[0]
-    cpad[EY : 2 * EY, 0:EZ] = coef_ref[1]
 
     barrier = pltpu.get_barrier_semaphore()
     expected = 0
@@ -368,8 +374,12 @@
         ref[(*index, 0, pl.ds(ROWS - YF, YF))] = total
         ref[(*index, 1, pl.ds(0, YF))] = total
 
+    load_coef.wait()
+    cpad[0:EY, 0:EZ] = coef[0]
+    cpad[EY : 2 * EY, 0:EZ] = coef[1]
+    load_rhs.wait()
     for e in range(EX):
-        Fr[0, e] = local_sum(rhs_ref[e])
+        Fr[0, e] = local_sum(Ar[e])
     middle(Fr, 0)
     sx[0, 0] = Fr[0, 0, 0:YF]
     sx[0, 1] = Fr[0, 1, ROWS - YF : ROWS]
@@ -479,43 +489,53 @@
     WFr[...] = edge(flane) * edge(fx) * edge(fy)
     WLFr[...] = edge(flane) * edge(fx, XF) * edge(fy, YF)
 
-    tile_exchange.arrive()
-    ext = tiles[...]
-    pd = rmul(ext, const["Bdf"], HOW["g"])
-    diag = lmul(const["Gdf"], pd[:, :ZF], pd[:, ZF:], n=HOW["g"])
-
     def mask_of(x, y, z, n):
         inner = (x > 0) & (x < gxn * EX * n - 1) & (y > 0) & (y < gyn * EY * n - 1)
         return inner & (z != 0) & (z != EZ * n - 1)
 
+    pd = rmul(cpad[...], const["Bdf"], HOW["g"])
+    diag = lmul(const["Gdo"], jnp.concatenate([pd[:, :ZF], pd[:, ZF:]], 0), n=HOW["g"])
     for e in range(EX):
         keep = mask_of(px * XF + e * N + xr, py * YF + yr, lanes, N)
         Dr[e] = jnp.where(keep, 1.0 / diag[e * ROWS : (e + 1) * ROWS], 0.0)
-    keep = mask_of(px * XF + fx, py * YF + fy, flane, N)
-    df = jnp.where(keep, 1.0 / diag[EX * ROWS :], 0.0)
+    fkeep = mask_of(px * XF + fx, py * YF + fy, flane, N)
+    tile_exchange.arrive()
+    pd = rmul(tiles[...], const["Bdf"], HOW["g"])
+    diag = lmul(const["Gdf"], pd[:, :ZF], pd[:, ZF:], n=HOW["g"])
+    df = jnp.where(fkeep, 1.0 / diag, 0.0)
     DFr[...] = df
     DcFr[...] = df * FXr[0]
-    pdc = rmul(ext, const["Bdc"], HOW["g"])
-    diag_c = lmul(const["Gdc"], pdc[:, :ZC], pdc[:, ZC:], n=HOW["g"])
-    crow = lax.broadcasted_iota(jnp.int32, (384, ZC), 0)
-    clane = lax.broadcasted_iota(jnp.int32, (384, ZC), 1)
-
-    def place(r, width, x0, y0):
-        return (x0 + r // width, y0 + lax.rem(r, width))
-
-    cx, cy = place(crow, YC, 0, 0)
-    base = OWN
-    for count, width, x0, y0 in (
-        (ROWS_C, YC, -NC, 0), (ROWS_C, YC, XC, 0), (XC * NC, NC, 0, -NC), (XC * NC, NC, 0, YC),
-        (16, NC, -NC, -NC), (16, NC, -NC, YC), (16, NC, XC, -NC), (16, NC, XC, YC),
-    ):
-        nx, ny = place(crow - base, width, x0, y0)
-        cx, cy = jnp.where(crow >= base, nx, cx), jnp.where(crow >= base, ny, cy)
-        base += count
-    keep = mask_of(px * XC + cx, py * YC + cy, clane, NC)
-    Dc_r[...] = jnp.where(keep, 1.0 / diag_c, 0.0)
-    lines = dot(jnp.concatenate(spread(ext), 1), const["Bs"][:, ZF:])
-    Cc_r[...] = dot(const["Pc"][...], jnp.concatenate(spread(lines), 0))
+    Dr[0, 0:YF] = df[0:YF]
+    Dr[1, ROWS - YF : ROWS] = df[YF : 2 * YF]
+    for x in range(XF):
+        e, r = x // N, (x % N) * YF
+        Dr[e, r : r + 1] = df[2 * YF + x : 2 * YF + x + 1]
+        b = 2 * YF + XF + x
+        Dr[e, r + YF - 1 : r + YF] = df[b : b + 1]
+
+    def coarse_setup():
+        ext = tiles[...]
+        pdc = rmul(ext, const["Bdc"], HOW["g"])
+        diag_c = lmul(const["Gdc"], pdc[:, :ZC], pdc[:, ZC:], n=HOW["g"])
+        crow = lax.broadcasted_iota(jnp.int32, (384, ZC), 0)
+        clane = lax.broadcasted_iota(jnp.int32, (384, ZC), 1)
+
+        def place(r, width, x0, y0):
+            return (x0 + r // width, y0 + lax.rem(r, width))
+
+        cx, cy = place(crow, YC, 0, 0)
+        base = OWN
+        for count, width, x0, y0 in (
+            (ROWS_C, YC, -NC, 0), (ROWS_C, YC, XC, 0), (XC * NC, NC, 0, -NC), (XC * NC, NC, 0, YC),
+            (16, NC, -NC, -NC), (16, NC, -NC, YC), (16, NC, XC, -NC), (16, NC, XC, YC),
+        ):
+            nx, ny = place(crow - base, width, x0, y0)
+            cx, cy = jnp.where(crow >= base, nx, cx), jnp.where(crow >= base, ny, cy)
+            base += count
+        keep = mask_of(px * XC + cx, py * YC + cy, clane, NC)
+        Dc_r[...] = jnp.where(keep, 1.0 / diag_c, 0.0)
+        lines = dot(jnp.concatenate(spread(ext), 1), const["Bs"][:, ZF:])
+        Cc_r[...] = dot(const["Pc"][...], jnp.concatenate(spread(lines), 0))
 
     def halo(i):
         fine(i).arrive()
@@ -584,10 +604,26 @@
     def cycle(k, carry):
         pl.when(k > 0)(lambda: finish(k - 1))
         bulk(lambda e: (Dr[e] * inv_center) * Fr[k, e], HOW["a"])
-        h = halo(4 * k)
-        ph = face_z(DcFr[...] * inv_center * h, HOW["a"])
-        send_faces(4 * k + 1, FXr[1] + face_to_face(ph, HOW["a"]))
-        add_faces(Fr, (k,), h)
+        @pl.when(k > 0)
+        def _():
+            h = halo(4 * k)
+            ph = face_z(DcFr[...] * inv_center * h, HOW["a"])
+            FXr[1] = FXr[1] + face_to_face(ph, HOW["a"])
+            PHr[...] = ph
+            Hr[...] = h
+
+        send_faces(4 * k + 1, FXr[1])
+
+        @pl.when(k > 0)
+        def _():
+            add_faces(Fr, (k,), Hr[...])
+            face_to_all(PHr[...], HOW["a"])
+
+        @pl.when(k == 0)
+        def _():
+            middle(Lr)
+            coarse_setup()
+
         FFr[k, 0:YF] = Fr[k, 0, 0:YF]
         FFr[k, YF : 2 * YF] = Fr[k, 1, ROWS - YF : ROWS]
         for x in range(XF):
@@ -595,7 +631,6 @@
             FFr[k, 2 * YF + x : 2 * YF + x + 1] = Fr[k, e, r : r + 1]
             b = 2 * YF + XF + x
             FFr[k, b : b + 1] = Fr[k, e, r + YF - 1 : r + YF]
-        face_to_all(ph, HOW["a"])
         gl = None
         for e in range(EX):
             s = Dr[e] * (a_f * Fr[k, e] - k_f * Lr[e])
@@ -665,6 +700,7 @@
         Hr[...] = h
         return carry
 
+    add_faces(Fr, (0,), halo(0))
     lax.fori_loop(0, 2, cycle, 0)
 
     def reduce_stage(buf, stage, base):
@@ -742,16 +778,16 @@
             vm(3, *field), vm(2, *field), vm(*field), vm(*field), vm(*field), vm(384, ZC), vm(*face), vm(*face),
             vm(*field), vm(*field), vm(*field), vm(*field), vm(2, *face), vm(2, *face), vm(96, 2 * ZF), vm(*face),
             vm(ROWS, ZF), vm(ROWS, ZF), vm(*face), vm(*face),
-            vm(384, ZC), vm(384, ZC), vm(8, 128), vm(80, 128),
+            vm(384, ZC), vm(384, ZC), vm(8, 128), vm(EX, EY, EZ), vm(80, 128),
             vm(9, 2, YF, ZF), vm(9, 2, EX * N, ZF), vm(9, 2, YF, ZF), vm(9, 2, EX * N, ZF), vm(9, 2, EX * N, ZF),
             vm(2, 192, ZC), vm(2, 256, ZC),
             vm(2, 8, 128), vm(gyn, 8, 128), vm(gxn, 8, 128),
-            dma(len(names)), dma(9, 8), dma(9, 8), dma(2, 8), dma(2, 8), dma(8), dma(8), dma(n_dots), dma(n_dots),
+            dma(len(names) + 2), dma(9, 8), dma(9, 8), dma(2, 8), dma(2, 8), dma(8), dma(8), dma(n_dots), dma(n_dots),
         ]
         sol, res = pl.pallas_call(
             functools.partial(kernel_body, (gxn, gyn), names),
             out_shape=[pltpu.VMEM(field, F32)] * 2,
-            in_specs=[pl.BlockSpec(memory_space=pltpu.VMEM)] * 2 + [pl.BlockSpec(memory_space=pl.ANY)] * len(names),
+            in_specs=[pl.BlockSpec(memory_space=pl.ANY)] * (2 + len(names)),
             out_specs=[pl.BlockSpec(memory_space=pltpu.VMEM)] * 2,
             scratch_shapes=scratch,
             compiler_params=pltpu.CompilerParams(

time: 75.4 us -> 73.3 us (0.972)
  Pallas kernels: 73 us -> 71 us
    pallas_call x1, Pallas kernels: 73 us -> 71 us  [per_device(): pl.pallas_call(functools.partial(kernel_body, (gxn, gyn), names), out_sha...]
where the time goes in v4:
time: 73.3 us; the launch traced here: 73.2 us
  Pallas kernels  71 us (97%)
  local copies, waits for them, and re-layouts  1.59 us (2%)
    pallas_call x1, Pallas kernels, per_device(): pl.pallas_call(functools.partial(kernel_body, (gxn, gyn), names), out_sha...  71 us
    unnamed x2, local copies, waits for them, and re-layouts  1.59 us

profile of v4, /device:TPU:1, one launch (start us, length us, event | category | flops | bytes accessed | tf_op | source)
XLA Modules:
  0.0 73.2 jit_solution(3342374670405634325)
XLA Ops:
  0.6 71.0 %shard_map.302 = (f32[2,256,256]{2,1,0:T(8,128)S(1)}, f32[2,256,256]{2,1,0:T(8,128)S(1)}) custom-call(f32[2,256,256]{2,1,0:T(8,128)} %bitcast.5, f32[2,4,32]{2,1,0:T(4,128)} %coef_ref.1, bf16[1536,512]{1,0:T(8,128)(2,1)} %constant.58.clone.refs_0_, bf16[256,1536]{1,0:T(8,128)(2,1)} %constant.59.clone.refs_1_, bf16[1536,256]{1,0:T(8,128)(2,1)} %constant.60.clone.refs_2_, ...), custom_call_target="tpu_custom_call" | custom-call | tf_op jit(solution)/shard_map/pallas_call | solution.py:787
  71.7 0.8 %copy.35 = f32[16,32,256]{2,1,0:T(8,128)} copy(f32[16,32,256]{2,1,0:T(8,128)S(1)} %bitcast.4) | data formatting | bytes 1048576
  72.4 0.8 %copy.36 = f32[16,32,256]{2,1,0:T(8,128)} copy(f32[16,32,256]{2,1,0:T(8,128)S(1)} %bitcast.3) | data formatting | bytes 1048576

commit v5 on v4

--- a/solution.py
+++ b/solution.py
@@ -187,7 +187,13 @@
     out["zu"] = wide(((z % N == N - 1) & (z != ZF - 1))[None, :], (8, ZF))
     out["zd"] = wide(((z % N == 0) & (z != 0))[None, :], (8, ZF))
     Sy = np.kron(np.eye(EX * N), sum_matrix(EY, N))
-    out["F2F"] = left3(np.concatenate([SM[F][:, F], SN[F][:, F]], 1))
+    out["Mff"] = left3(blocks(EX, M0 / wxy[:, None])[F][:, F])
+    out["Kz1"] = right3((Kz / wz[None, :])[:128, :128])
+    out["w3f"] = (np.tile(wxy, EX)[F][:, None] * wz[None, :]).astype(np.float32)
+    along = np.concatenate([np.arange(YF), np.arange(YF), np.arange(EX * N), np.arange(EX * N)])
+    ends = np.concatenate([np.full(2 * YF, YF), np.full(2 * EX * N, EX * N)])
+    out["fu"] = wide(((along % N == N - 1) & (along != ends - 1))[:, None], (96, 128))
+    out["fd"] = wide(((along % N == 0) & (along != 0))[:, None], (96, 128))
     for e in range(EX):
         rows = slice(e * ROWS, (e + 1) * ROWS)
         here = np.concatenate([np.arange(e * YF, (e + 1) * YF), np.arange(2 * YF, len(F))])
@@ -228,9 +234,10 @@
     out["Pc"] = np.concatenate([pick.astype(np.float32).astype(BF16)] * 3, 1)
     Jxy = blocks(EX, np.kron(J, blocks(EY, J)))
     out["Bj"] = right3(np.concatenate([JZ.T @ Wz @ Sz, JZ.T @ Kz @ Sz, JZ.T], 1), "d")
-    sel = np.concatenate([np.arange(EX * ROWS), F])
-    JM, JN = (SM @ Jxy)[sel], (SN @ Jxy)[sel]
+    out["Bjv"] = right3(np.concatenate([JZ.T @ Wz @ Sz, JZ.T @ Kz @ Sz], 0), "d")
+    JM, JN = SM @ Jxy, SN @ Jxy
     out["Gj"] = left3(np.concatenate([JM, JN], 1), "d")
+    out["Gjf"] = left3(np.concatenate([JM[F], JN[F]], 0), "d")
     out["Gp"] = left3(Jxy, "d")
     fine_x, fine_y = np.divmod(np.arange(EX * ROWS), YF)
     places = {"f": (np.concatenate([fine_x, F // YF]), np.concatenate([fine_y, F % YF])), "c": (cx, cy)}
@@ -307,7 +314,7 @@
     sol_ref, res_ref = refs[n_const : n_const + 2]
     rest = refs[n_const + 2 :]
     const = dict(zip(names, rest[:n_const]))
-    (Fr, Zr, Dr, Cr, W3r, gr, DFr, DcFr, Lr, Sr, Rr, Ar, FXr, FFr, PHr, Hr, Wr, WLr, WFr, WLFr,
+    (Fr, Zr, Dr, Cr, W3r, W3Fr, Er, gr, DFr, DcFr, Lr, Sr, Rr, Ar, FXr, FFr, Hr, Wr, WLr, WFr, WLFr,
      Dc_r, Cc_r, cpad, coef, tiles,
      sx, sy, rx, ry, rc, cs, cr, dots, d1, d2,
      const_sem, send_sem, recv_sem, csend_sem, crecv_sem, tsend_sem, trecv_sem, dsend_sem, drecv_sem) = rest[n_const:]
@@ -330,9 +337,19 @@
 
     corners = [(dx, dy) for dx in (-1, 1) for dy in (-1, 1)]
     around = corners + [(-1, 0), (1, 0), (0, -1), (0, 1)]
+    def ring(coarse_n, fine_n, hops):
+        every = [(a, b) for a in range(coarse_n) for b in range(fine_n) if (a, b) != (0, 0)]
+        near = lambda d, n: min(d, n - d)
+        return sorted(every, key=lambda o: -(near(o[0], coarse_n) + hops * near(o[1], fine_n)))
+
+    def shifted(p, fine_n, coarse_n, o):
+        return lax.rem(p // fine_n + o[0], coarse_n) * fine_n + lax.rem(lax.rem(p, fine_n) + o[1], fine_n)
+
+    nz = 8 if gxn % 8 == 0 else 2
+    nx, ny = gyn // 2, gxn // nz
     stages = [
-        [(px, lax.rem(py + d, gyn)) for d in range(1, gyn)],
-        [(lax.rem(px + d, gxn), py) for d in range(1, gxn)],
+        [(px, shifted(py, 2, nx, o)) for o in ring(nx, 2, 0.5)],
+        [(shifted(px, nz, ny, o), py) for o in ring(ny, nz, 1)],
     ]
 
     copies = [pltpu.make_async_copy(const_hbm[m], const[m], const_sem.at[i]) for i, m in enumerate(names)]
@@ -471,6 +488,8 @@
         FXr[0, e * YF : (e + 1) * YF] = one
         FXr[0, 2 * YF + e * N : 2 * YF + (e + 1) * N] = cf[0]
         FXr[0, 2 * YF + (EX + e) * N : 2 * YF + (EX + e + 1) * N] = cf[EY - 1]
+
+    W3Fr[...] = FXr[0] * const["w3f"][...]
 
     rows = lax.broadcasted_iota(jnp.int32, (ROWS, ZF), 0)
     lanes = lax.broadcasted_iota(jnp.int32, (ROWS, ZF), 1)
@@ -582,8 +601,21 @@
         sy[i, 1] = faces[2 * YF + XF :]
         fine(i).start()
 
-    def face_to_face(ph, n):
-        return lmul(const["F2F"], ph[:, :ZF], ph[:, ZF:], n=n)
+    def face_to_face(delta, n):
+        p = split(delta, n)
+        p = [p[i] for i, _ in TERMS[:n]]
+        t = dot(const["Mff"][:, : n * 96], jnp.concatenate(p, 0))
+        halves = [jnp.concatenate([q[:, :128], q[:, 128:]], 0) for q in p]
+        r = dot(jnp.concatenate(halves, 1), const["Kz1"][: n * 128])
+        Er[...] = jnp.concatenate([r[:96], r[96:]], 1)
+        for a, b in ((0, 2 * YF), (YF - 1, 2 * YF + XF), (YF, 2 * YF + XF - 1), (2 * YF - 1, 2 * YF + 2 * XF - 1)):
+            both = Er[a : a + 1] + Er[b : b + 1]
+            Er[a : a + 1] = both
+            Er[b : b + 1] = both
+        v = W3Fr[...] * (t + Er[...])
+        wide = lambda name: jnp.concatenate([const[name][...]] * 2, 1)
+        v = v + wide("fu") * pltpu.roll(v, 95, 0) + wide("fd") * pltpu.roll(v, 1, 0)
+        return v + const["zu"][0:1] * pltpu.roll(v, ZF - 1, 1) + const["zd"][0:1] * pltpu.roll(v, 1, 1)
 
     def face_to_all(ph, n):
         for e in range(EX):
@@ -593,7 +625,7 @@
 
     def finish(k):
         add_faces(Zr, (k,), (-k_f) * DFr[...] * Hr[...])
-        face_to_all(PHr[...], HOW["h"])
+        face_to_all(face_z((-k_f) * DcFr[...] * Hr[...], HOW["h"]), HOW["h"])
         for e in range(EX):
             Fr[k + 1, e] = Lr[e]
 
@@ -607,9 +639,7 @@
         @pl.when(k > 0)
         def _():
             h = halo(4 * k)
-            ph = face_z(DcFr[...] * inv_center * h, HOW["a"])
-            FXr[1] = FXr[1] + face_to_face(ph, HOW["a"])
-            PHr[...] = ph
+            FXr[1] = FXr[1] + face_to_face(DFr[...] * inv_center * h, HOW["a"])
             Hr[...] = h
 
         send_faces(4 * k + 1, FXr[1])
@@ -617,7 +647,7 @@
         @pl.when(k > 0)
         def _():
             add_faces(Fr, (k,), Hr[...])
-            face_to_all(PHr[...], HOW["a"])
+            face_to_all(face_z(DcFr[...] * inv_center * Hr[...], HOW["a"]), HOW["a"])
 
         @pl.when(k == 0)
         def _():
@@ -650,7 +680,7 @@
         bulk(lambda e: Sr[e], HOW["s"])
         ph = face_z(hs, HOW["s"])
         face_to_all(ph, HOW["s"])
-        FXr[1] = FXr[1] + face_to_face(ph, HOW["s"])
+        FXr[1] = FXr[1] + face_to_face((-k_f) * DFr[...] * h, HOW["s"])
         add_faces(Sr, (), (-k_f) * DFr[...] * h)
         coarse(k).arrive()
         gr[OWN:] = cr[k]
@@ -662,10 +692,12 @@
         o = rmul(jnp.concatenate([p[:OWN], p[OWN:]], 1), const["Bc"], HOW["c"])
         g = gr[0:OWN]
         fix = Dc_r[0:OWN] * (a_c * g - k_c * o)
-        p = rmul(Cc_r[0:OWN] * fix, const["Bj"], HOW["d"], slice(0, 2 * ZF))
-        o = lmul(const["Gj"], p[:, :ZF], p[:, ZF:], n=HOW["d"], rows=slice(EX * ROWS, EX * ROWS + 96))
+        fix_c = Cc_r[0:OWN] * fix
+        p = lmul(const["Gjf"], fix_c, n=HOW["d"])
+        o = rmul(jnp.concatenate([p[:96], p[96:]], 1), const["Bjv"], HOW["d"])
         send_faces(4 * k + 2, FXr[1] + o)
-        o = lmul(const["Gj"], p[:, :ZF], p[:, ZF:], n=HOW["d"], rows=slice(0, EX * ROWS))
+        p = rmul(fix_c, const["Bj"], HOW["d"], slice(0, 2 * ZF))
+        o = lmul(const["Gj"], p[:, :ZF], p[:, ZF:], n=HOW["d"])
         p = rmul(fix, const["Bj"], HOW["d"], slice(2 * ZF, 3 * ZF))
         up = lmul(const["Gp"], p, n=HOW["d"])
         for e in range(EX):
@@ -674,10 +706,9 @@
             Rr[e] = Fr[k, e] - Lr[e] - o[part]
         bulk(lambda e: (Dr[e] * inv_center) * Rr[e], HOW["e"])
         h = halo(4 * k + 2)
-        ph = face_z((-inv_center) * DcFr[...] * h, HOW["e"])
-        send_faces(4 * k + 3, FXr[1] + face_to_face(ph, HOW["e"]))
+        send_faces(4 * k + 3, FXr[1] + face_to_face((-inv_center) * DFr[...] * h, HOW["e"]))
         add_faces(Rr, (), -h)
-        face_to_all(ph, HOW["e"])
+        face_to_all(face_z((-inv_center) * DcFr[...] * h, HOW["e"]), HOW["e"])
         for e in range(EX):
             Zr[k, e] = Sr[e] + Dr[e] * (a_f * Rr[e] - k_f * Lr[e])
         bulk(lambda e: Zr[k, e], HOW["f"])
@@ -689,14 +720,12 @@
                 sums[i] = sums[i] + total(t)
         h = halo(4 * k + 3)
         delta = (-k_f) * DFr[...] * h
-        ph = face_z((-k_f) * DcFr[...] * h, HOW["h"])
-        ff = face_to_face(ph, HOW["h"])
+        ff = face_to_face(delta, HOW["h"])
         send_faces(4 * k + 4, FXr[1] + ff)
         wd = WFr[...] * delta
         faces = (FFr[0] * wd, FFr[k] * wd, WLFr[...] * delta * (2.0 * FXr[1] + ff))
         for i, t in enumerate(faces):
             dots[k, i : i + 1] = sums[i] + total(t)
-        PHr[...] = ph
         Hr[...] = h
         return carry
 
@@ -761,6 +790,15 @@
         coarse(k).drain()
 
 
+def store(sol_ref, res_ref, sol_out, res_out, sem):
+    pairs = [(a.at[e], b.at[e]) for e in range(EX) for a, b in ((sol_ref, sol_out), (res_ref, res_out))]
+    copies = [pltpu.make_async_copy(a, b, sem.at[i]) for i, (a, b) in enumerate(pairs)]
+    for c in copies:
+        c.start()
+    for c in copies:
+        c.wait()
+
+
 def solution(mesh):
     gxn, gyn = mesh.shape["gx"], mesh.shape["gy"]
     table = constants()
@@ -775,8 +813,8 @@
         face = (96, ZF)
         scratch = [pltpu.VMEM(table[m].shape, table[m].dtype) for m in names]
         scratch += [
-            vm(3, *field), vm(2, *field), vm(*field), vm(*field), vm(*field), vm(384, ZC), vm(*face), vm(*face),
-            vm(*field), vm(*field), vm(*field), vm(*field), vm(2, *face), vm(2, *face), vm(96, 2 * ZF), vm(*face),
+            vm(3, *field), vm(2, *field), vm(*field), vm(*field), vm(*field), vm(*face), vm(*face), vm(384, ZC), vm(*face), vm(*face),
+            vm(*field), vm(*field), vm(*field), vm(*field), vm(2, *face), vm(2, *face), vm(*face),
             vm(ROWS, ZF), vm(ROWS, ZF), vm(*face), vm(*face),
             vm(384, ZC), vm(384, ZC), vm(8, 128), vm(EX, EY, EZ), vm(80, 128),
             vm(9, 2, YF, ZF), vm(9, 2, EX * N, ZF), vm(9, 2, YF, ZF), vm(9, 2, EX * N, ZF), vm(9, 2, EX * N, ZF),
@@ -794,6 +832,13 @@
                 collective_id=0, has_side_effects=True, vmem_limit_bytes=56 * 2**20
             ),
         )(rhs, coefficient, *[jnp.asarray(table[m]) for m in names])
+        sol, res = pl.pallas_call(
+            store,
+            out_shape=[jax.ShapeDtypeStruct(field, F32)] * 2,
+            in_specs=[pl.BlockSpec(memory_space=pltpu.VMEM)] * 2,
+            out_specs=[pl.BlockSpec(memory_space=pl.ANY)] * 2,
+            scratch_shapes=[pltpu.SemaphoreType.DMA((4,))],
+        )(sol, res)
         return sol.reshape(right_side.shape), res.reshape(right_side.shape)
 
     spec = P("gx", "gy", None)

time: 73.3 us -> 74.4 us (1.015)
  Pallas kernels: 71 us -> 72.1 us
    pallas_call x0 -> x1, Pallas kernels: none -> 2.19 us  [per_device(): pl.pallas_call(store, out_shape=[jax.ShapeDtypeStruct(field, F32)] * 2, i...]
    pallas_call x1, Pallas kernels: 71 us -> 69.9 us  [per_device(): pl.pallas_call(functools.partial(kernel_body, (gxn, gyn), names), out_sha...]
    unnamed x2 -> x4, local copies, waits for them, and re-layouts: 1.59 us -> 1.56 us
where the time goes in v5:
time: 74.4 us; the launch traced here: 74.3 us
  Pallas kernels  72.1 us (97%)
  local copies, waits for them, and re-layouts  1.56 us (2%)
    pallas_call x1, Pallas kernels, per_device(): pl.pallas_call(functools.partial(kernel_body, (gxn, gyn), names), out_sha...  69.9 us
    pallas_call x1, Pallas kernels, per_device(): pl.pallas_call(store, out_shape=[jax.ShapeDtypeStruct(field, F32)] * 2, i...  2.19 us
    unnamed x4, local copies, waits for them, and re-layouts  1.56 us

profile of v5, /device:TPU:1, one launch (start us, length us, event | category | flops | bytes accessed | tf_op | source)
XLA Modules:
  0.0 74.3 jit_solution(14387172734398002971)
XLA Ops:
  0.6 69.9 %shard_map.356 = (f32[2,256,256]{2,1,0:T(8,128)S(1)}, f32[2,256,256]{2,1,0:T(8,128)S(1)}) custom-call(f32[2,256,256]{2,1,0:T(8,128)} %bitcast.3, f32[2,4,32]{2,1,0:T(4,128)} %coef_ref.1, bf16[1536,512]{1,0:T(8,128)(2,1)} %constant.70.clone.refs_0_, bf16[256,1536]{1,0:T(8,128)(2,1)} %constant.71.clone.refs_1_, bf16[1536,256]{1,0:T(8,128)(2,1)} %constant.72.clone.refs_2_, ...), custom_call_target="tpu_custom_call" | custom-call | tf_op jit(solution)/shard_map/pallas_call | solution.py:825
  70.5 0.0 copy-start
  70.5 0.8 %copy-done = f32[2,256,256]{2,1,0:T(8,128)} copy-done((f32[2,256,256]{2,1,0:T(8,128)}, f32[2,256,256]{2,1,0:T(8,128)S(1)}, u32[]{:S(2)}) %copy-start) | copy-done | bytes 524312
  71.3 0.0 copy-start.1
  71.3 0.8 %copy-done.1 = f32[2,256,256]{2,1,0:T(8,128)} copy-done((f32[2,256,256]{2,1,0:T(8,128)}, f32[2,256,256]{2,1,0:T(8,128)S(1)}, u32[]{:S(2)}) %copy-start.1) | copy-done | bytes 524312
  72.1 2.2 %shard_map.357 = (f32[2,256,256]{2,1,0:T(8,128)}, f32[2,256,256]{2,1,0:T(8,128)}) custom-call(f32[2,256,256]{2,1,0:T(8,128)} %copy-done, f32[2,256,256]{2,1,0:T(8,128)} %copy-done.1), custom_call_target="tpu_custom_call" | custom-call | tf_op jit(solution)/shard_map/pallas_call | solution.py:835
Async XLA Ops:
  70.5 0.8 %copy-start = (f32[2,256,256]{2,1,0:T(8,128)}, f32[2,256,256]{2,1,0:T(8,128)S(1)}, u32[]{:S(2)}) copy-start(f32[2,256,256]{2,1,0:T(8,128)S(1)} %get-tuple-element.6.sol_ref) | copy-start | bytes 1572868
  71.3 0.8 %copy-start.1 = (f32[2,256,256]{2,1,0:T(8,128)}, f32[2,256,256]{2,1,0:T(8,128)S(1)}, u32[]{:S(2)}) copy-start(f32[2,256,256]{2,1,0:T(8,128)S(1)} %get-tuple-element.7.res_ref) | copy-start | bytes 1572868

commit v6 on v5

--- a/solution.py
+++ b/solution.py
@@ -405,6 +405,8 @@
         sy[0, 0, x : x + 1] = Fr[0, e, r : r + 1]
         sy[0, 1, x : x + 1] = Fr[0, e, r + YF - 1 : r + YF]
 
+    interior = inside(-1, -1) & inside(1, 1)
+
     class Exchange:
         def __init__(self, plan, send, recv):
             self.plan = [
@@ -415,12 +417,26 @@
             ]
 
         def start(self):
-            for c, to, _ in self.plan:
-                pl.when(to)(c.start)
+            @pl.when(interior)
+            def _():
+                for c, _, _ in self.plan:
+                    c.start()
+
+            @pl.when(~interior)
+            def _():
+                for c, to, _ in self.plan:
+                    pl.when(to)(c.start)
 
         def arrive(self):
-            for c, _, come in self.plan:
-                pl.when(come)(c.wait_recv)
+            @pl.when(interior)
+            def _():
+                for c, _, _ in self.plan:
+                    c.wait_recv()
+
+            @pl.when(~interior)
+            def _():
+                for c, _, come in self.plan:
+                    pl.when(come)(c.wait_recv)
 
         def drain(self):
             for c, to, _ in self.plan:
@@ -760,6 +776,17 @@
     d2[0] = summed(d1, stage1, len(stage1))
     for c in stage2:
         c.start()
+    tile_exchange.drain()
+    for c in stage1:
+        c.wait_send()
+
+    def drain(i, carry):
+        fine(i).drain()
+        return carry
+
+    lax.fori_loop(0, 9, drain, 0)
+    for k in range(2):
+        coarse(k).drain()
     h = halo(8)
     add_faces(Fr, (2,), h)
     lanes_sum = jnp.sum(summed(d2, stage2, len(stage2)), axis=1, keepdims=True)
@@ -776,27 +803,8 @@
     for e in range(EX):
         sol_ref[e] = c_z * Zr[0, e] - c_u * Zr[1, e]
         res_ref[e] = jnp.where(Dr[e] > 0.0, Fr[0, e] - c_z * Fr[1, e] + c_u * Fr[2, e], 0.0)
-
-    tile_exchange.drain()
-    for c in stage1 + stage2:
+    for c in stage2:
         c.wait_send()
-
-    def drain(i, carry):
-        fine(i).drain()
-        return carry
-
-    lax.fori_loop(0, 9, drain, 0)
-    for k in range(2):
-        coarse(k).drain()
-
-
-def store(sol_ref, res_ref, sol_out, res_out, sem):
-    pairs = [(a.at[e], b.at[e]) for e in range(EX) for a, b in ((sol_ref, sol_out), (res_ref, res_out))]
-    copies = [pltpu.make_async_copy(a, b, sem.at[i]) for i, (a, b) in enumerate(pairs)]
-    for c in copies:
-        c.start()
-    for c in copies:
-        c.wait()
 
 
 def solution(mesh):
@@ -832,13 +840,6 @@
                 collective_id=0, has_side_effects=True, vmem_limit_bytes=56 * 2**20
             ),
         )(rhs, coefficient, *[jnp.asarray(table[m]) for m in names])
-        sol, res = pl.pallas_call(
-            store,
-            out_shape=[jax.ShapeDtypeStruct(field, F32)] * 2,
-            in_specs=[pl.BlockSpec(memory_space=pltpu.VMEM)] * 2,
-            out_specs=[pl.BlockSpec(memory_space=pl.ANY)] * 2,
-            scratch_shapes=[pltpu.SemaphoreType.DMA((4,))],
-        )(sol, res)
         return sol.reshape(right_side.shape), res.reshape(right_side.shape)
 
     spec = P("gx", "gy", None)

time: 74.4 us -> 72.1 us (0.969)
  Pallas kernels: 72.1 us -> 69.8 us
    pallas_call x1 -> x0, Pallas kernels: 2.19 us -> none  [per_device(): pl.pallas_call(store, out_shape=[jax.ShapeDtypeStruct(field, F32)] * 2, i...]
    unnamed x4 -> x2, local copies, waits for them, and re-layouts: 1.56 us -> 1.59 us
where the time goes in v6:
time: 72.1 us; the launch traced here: 72 us
  Pallas kernels  69.8 us (97%)
  local copies, waits for them, and re-layouts  1.59 us (2%)
    pallas_call x1, Pallas kernels, per_device(): pl.pallas_call(functools.partial(kernel_body, (gxn, gyn), names), out_sha...  69.8 us
    unnamed x2, local copies, waits for them, and re-layouts  1.59 us

profile of v6, /device:TPU:1, one launch (start us, length us, event | category | flops | bytes accessed | tf_op | source)
XLA Modules:
  0.0 72.0 jit_solution(2384630644886602658)
XLA Ops:
  0.6 69.8 %shard_map.356 = (f32[2,256,256]{2,1,0:T(8,128)S(1)}, f32[2,256,256]{2,1,0:T(8,128)S(1)}) custom-call(f32[2,256,256]{2,1,0:T(8,128)} %bitcast.5, f32[2,4,32]{2,1,0:T(4,128)} %coef_ref.1, bf16[1536,512]{1,0:T(8,128)(2,1)} %constant.70.clone.refs_0_, bf16[256,1536]{1,0:T(8,128)(2,1)} %constant.71.clone.refs_1_, bf16[1536,256]{1,0:T(8,128)(2,1)} %constant.72.clone.refs_2_, ...), custom_call_target="tpu_custom_call" | custom-call | tf_op jit(solution)/shard_map/pallas_call | solution.py:833
  70.5 0.8 %copy.41 = f32[16,32,256]{2,1,0:T(8,128)} copy(f32[16,32,256]{2,1,0:T(8,128)S(1)} %bitcast.4) | data formatting | bytes 1048576
  71.3 0.8 %copy.42 = f32[16,32,256]{2,1,0:T(8,128)} copy(f32[16,32,256]{2,1,0:T(8,128)S(1)} %bitcast.3) | data formatting | bytes 1048576

commit v7 on v6

--- a/solution.py
+++ b/solution.py
@@ -357,23 +357,23 @@
     load_coef = pltpu.make_async_copy(coef_ref, coef, const_sem.at[n_const + 1])
     load_rhs.start()
     load_coef.start()
-    for c in copies:
-        c.start()
 
     for ref in (rx, ry, rc, cr, tiles, cpad):
         ref[...] = jnp.zeros_like(ref)
 
     barrier = pltpu.get_barrier_semaphore()
     expected = 0
+    for stage in stages[::-1]:
+        for p in stage:
+            pl.semaphore_signal(barrier, inc=1, device_id=p, device_id_type=MESH)
+        expected = expected + len(stage)
     for d in around:
         pl.when(inside(*d))(
             lambda d=d: pl.semaphore_signal(barrier, inc=1, device_id=at(*d), device_id_type=MESH)
         )
         expected = expected + inside(*d).astype(jnp.int32)
-    for stage in stages:
-        for p in stage:
-            pl.semaphore_signal(barrier, inc=1, device_id=p, device_id_type=MESH)
-        expected = expected + len(stage)
+    for c in copies:
+        c.start()
 
     def local_sum(v):
         rows = lax.broadcasted_iota(jnp.int32, v.shape, 0)
@@ -737,7 +737,8 @@
         h = halo(4 * k + 3)
         delta = (-k_f) * DFr[...] * h
         ff = face_to_face(delta, HOW["h"])
-        send_faces(4 * k + 4, FXr[1] + ff)
+        Er[...] = FXr[1] + ff
+        pl.when(k == 0)(lambda: send_faces(4 * k + 4, Er[...]))
         wd = WFr[...] * delta
         faces = (FFr[0] * wd, FFr[k] * wd, WLFr[...] * delta * (2.0 * FXr[1] + ff))
         for i, t in enumerate(faces):
@@ -772,6 +773,7 @@
     stage2 = reduce_stage(d2, stages[1], len(stage1))
     for c in stage1:
         c.start()
+    send_faces(8, Er[...])
     finish(1)
     d2[0] = summed(d1, stage1, len(stage1))
     for c in stage2:
@@ -802,7 +804,7 @@
     c_u = alpha1 * alpha0
     for e in range(EX):
         sol_ref[e] = c_z * Zr[0, e] - c_u * Zr[1, e]
-        res_ref[e] = jnp.where(Dr[e] > 0.0, Fr[0, e] - c_z * Fr[1, e] + c_u * Fr[2, e], 0.0)
+        res_ref[e] = Fr[0, e] - c_z * Fr[1, e] + c_u * Fr[2, e]
     for c in stage2:
         c.wait_send()
 
@@ -840,7 +842,14 @@
                 collective_id=0, has_side_effects=True, vmem_limit_bytes=56 * 2**20
             ),
         )(rhs, coefficient, *[jnp.asarray(table[m]) for m in names])
-        return sol.reshape(right_side.shape), res.reshape(right_side.shape)
+        def inner(dim, axis, n):
+            i = lax.broadcasted_iota(jnp.int32, right_side.shape, dim)
+            here = lax.axis_index(axis) * right_side.shape[dim] if axis else 0
+            return (i != -here) & (i != n * right_side.shape[dim] - 1 - here)
+
+        keep = inner(0, "gx", gxn) & inner(1, "gy", gyn) & inner(2, None, 1)
+        zeroed = lambda x: jnp.where(keep, x.reshape(right_side.shape), 0.0)
+        return zeroed(sol), zeroed(res)
 
     spec = P("gx", "gy", None)
     return jax.shard_map(

time: 72.1 us -> 71.5 us (level)
  local copies, waits for them, and re-layouts: 1.59 us -> 0 us
  other arithmetic: 0 us -> 1.22 us
    unnamed x2 -> x0, local copies, waits for them, and re-layouts: 1.59 us -> none
    select_n x0 -> x1, other arithmetic: none -> 1.2 us  [per_device(): zeroed = lambda x: jnp.where(keep, x.reshape(right_side.shape), 0.0)]
where the time goes in v7:
time: 71.5 us; the launch traced here: 71.4 us
  Pallas kernels  69.5 us (97%)
  other arithmetic  1.22 us (2%)
    pallas_call x1, Pallas kernels, per_device(): pl.pallas_call(functools.partial(kernel_body, (gxn, gyn), names), out_sha...  69.5 us

profile of v7, /device:TPU:1, one launch (start us, length us, event | category | flops | bytes accessed | tf_op | source)
XLA Modules:
  0.0 71.4 jit_solution(2585316622202800425)
XLA Ops:
  0.7 69.5 %shard_map.356 = (f32[2,256,256]{2,1,0:T(8,128)S(1)}, f32[2,256,256]{2,1,0:T(8,128)S(1)}) custom-call(f32[2,256,256]{2,1,0:T(8,128)} %bitcast.5, f32[2,4,32]{2,1,0:T(4,128)} %coef_ref.1, bf16[1536,512]{1,0:T(8,128)(2,1)} %constant.92.clone.refs_0_, bf16[256,1536]{1,0:T(8,128)(2,1)} %constant.93.clone.refs_1_, bf16[1536,256]{1,0:T(8,128)(2,1)} %constant.94.clone.refs_2_, ...), custom_call_target="tpu_custom_call" | custom-call | tf_op jit(solution)/shard_map/pallas_call | solution.py:835
  70.2 1.2 %fusion = (f32[16,32,256]{2,1,0:T(8,128)}, f32[16,32,256]{2,1,0:T(8,128)}) fusion(f32[16,32,256]{2,1,0:T(8,128)S(1)} %bitcast.4, pred[256]{0:T(512)(128)(4,1)S(1)} %compare_and_fusion, pred[32]{0:T(512)(128)(4,1)S(1)} %compare_and_fusion.1, pred[16]{0:T(512)(128)(4,1)S(1)} %compare_and_fusion.2, f32[16,32,256]{2,1,0:T(8,128)S(1)} %bitcast.3), kind=kLoop, calls=%fused_computation.1 | loop fusion | flops 524288 | bytes 2097456 | tf_op jit(solution)/shard_map/jit(_where)/select_n | solution.py:851
  (3 shorter events, 0.0 us)

commit v8 on v7

--- a/solution.py
+++ b/solution.py
@@ -358,8 +358,14 @@
     load_rhs.start()
     load_coef.start()
 
-    for ref in (rx, ry, rc, cr, tiles, cpad):
-        ref[...] = jnp.zeros_like(ref)
+    interior = inside(-1, -1) & inside(1, 1)
+    rc[...] = jnp.zeros_like(rc)
+
+    @pl.when(~interior)
+    def _():
+        for ref in (rx, ry, cr, tiles):
+            ref[...] = jnp.zeros_like(ref)
+
 
     barrier = pltpu.get_barrier_semaphore()
     expected = 0
@@ -391,6 +397,7 @@
         ref[(*index, 0, pl.ds(ROWS - YF, YF))] = total
         ref[(*index, 1, pl.ds(0, YF))] = total
 
+    cpad[...] = jnp.zeros_like(cpad)
     load_coef.wait()
     cpad[0:EY, 0:EZ] = coef[0]
     cpad[EY : 2 * EY, 0:EZ] = coef[1]
@@ -404,8 +411,6 @@
         e, r = x // N, (x % N) * YF
         sy[0, 0, x : x + 1] = Fr[0, e, r : r + 1]
         sy[0, 1, x : x + 1] = Fr[0, e, r + YF - 1 : r + YF]
-
-    interior = inside(-1, -1) & inside(1, 1)
 
     class Exchange:
         def __init__(self, plan, send, recv):

time: 71.5 us -> 71.5 us (level)
  no operation moved by 1% of the time
where the time goes in v8:
time: 71.5 us; the launch traced here: 71.4 us
  Pallas kernels  69.5 us (97%)
  other arithmetic  1.22 us (2%)
    pallas_call x1, Pallas kernels, per_device(): pl.pallas_call(functools.partial(kernel_body, (gxn, gyn), names), out_sha...  69.5 us

profile of v8, /device:TPU:1, one launch (start us, length us, event | category | flops | bytes accessed | tf_op | source)
XLA Modules:
  0.0 71.4 jit_solution(11144156738473068168)
XLA Ops:
  0.7 69.5 %shard_map.356 = (f32[2,256,256]{2,1,0:T(8,128)S(1)}, f32[2,256,256]{2,1,0:T(8,128)S(1)}) custom-call(f32[2,256,256]{2,1,0:T(8,128)} %bitcast.5, f32[2,4,32]{2,1,0:T(4,128)} %coef_ref.1, bf16[1536,512]{1,0:T(8,128)(2,1)} %constant.92.clone.refs_0_, bf16[256,1536]{1,0:T(8,128)(2,1)} %constant.93.clone.refs_1_, bf16[1536,256]{1,0:T(8,128)(2,1)} %constant.94.clone.refs_2_, ...), custom_call_target="tpu_custom_call" | custom-call | tf_op jit(solution)/shard_map/pallas_call | solution.py:840
  70.2 1.2 %fusion = (f32[16,32,256]{2,1,0:T(8,128)}, f32[16,32,256]{2,1,0:T(8,128)}) fusion(f32[16,32,256]{2,1,0:T(8,128)S(1)} %bitcast.4, pred[256]{0:T(512)(128)(4,1)S(1)} %compare_and_fusion, pred[32]{0:T(512)(128)(4,1)S(1)} %compare_and_fusion.1, pred[16]{0:T(512)(128)(4,1)S(1)} %compare_and_fusion.2, f32[16,32,256]{2,1,0:T(8,128)S(1)} %bitcast.3), kind=kLoop, calls=%fused_computation.1 | loop fusion | flops 524288 | bytes 2097456 | tf_op jit(solution)/shard_map/jit(_where)/select_n | solution.py:856
  (3 shorter events, 0.0 us)
